TPU v7x, 512 devices: a whole 4x4x16 slice. The times are simulated.
512 devices in a mesh: box: 32 (over y, x, core), dir: 16 (over z).
Axes of the slice: x: 4, y: 4, z: 16, core: 2. Of those that a mesh axis runs over, the one named last changes fastest.
Arguments:
- current: float32 [2, 1024, 128], P(None, 'box'), may hold values from -6 to 6
- near_block: float32 [2, 1024, 6, 128, 128], P(None, 'box', None, 'dir'), may hold values from -0.15625 to 0.15625
- neighbours: int32 [1024, 6], P('box'), may hold values from 0 to 1023, as said below
- near_count: int32 [1024], P('box'), may hold values from 1 to 6
- radiation: float32 [2, 2, 1024, 128, 512], P(None, None, 'box', 'dir'), may hold values from -0.1875 to 0.1875
- stencil: int32 [2048, 4], P('dir'), may hold values from 0 to 511, as said below
- stencil_weight: float32 [2048, 4], P('dir'), may hold values from -3 to 3
- child_shift: float32 [2, 8, 2048], P(None, None, 'dir'), may hold values from -4 to 4
- list_source: int32 [128, 16], replicated, may hold values from 0 to 127
- list_kind: int32 [128, 16], replicated, may hold values from 0 to 7
- list_count: int32 [128], replicated, may hold values from 1 to 16
- translation: float32 [2, 8, 2048], P(None, None, 'dir'), may hold values from -0.4 to 0.4
Outputs:
- field: float32 [2, 1024, 128], P(None, 'box', 'dir')
Inputs may be any that keep to these rules, and one draw needn't show every extreme that they name: `neighbours`: slot 0 of each leaf box is the box itself; every entry lies within 32 leaf boxes of its row's box. `stencil`: entry (q, i) lies between one below and two above q * 512 // 2048, taken modulo 512.
All inputs are finite; a program needn't handle non-finite values.
Results may differ from a plain program's by a relative error of at most 0.0003.
Values sent between devices are 32-bit elements; how exact they have to be, the bound alone decides.
No kernel may reach another device: no remote copies, remote signals or barrier semaphores. Data moves between devices by JAX's collectives and lax.ppermute only.
A program may use at most 64 MiB of HBM per device.

v0:
```python
import jax
import jax.numpy as jnp
from jax import lax
from jax.sharding import PartitionSpec as P

highest = lax.Precision.HIGHEST


def with_halo(block, sides, width):
    for axis, dim in sides:
        count = lax.axis_size(axis)
        forward = [(i, i + 1) for i in range(count - 1)]
        backward = [(target, source) for source, target in forward]
        low = lax.ppermute(
            lax.slice_in_dim(block, block.shape[dim] - width, None, axis=dim), axis, forward
        )
        high = lax.ppermute(lax.slice_in_dim(block, 0, width, axis=dim), axis, backward)
        block = jnp.concatenate([low, block, high], axis=dim)
    return block


def complex_apply(form, left_re, left_im, right_re, right_im):
    real_part = jnp.einsum(form, left_re, right_re, precision=highest) - jnp.einsum(
        form, left_im, right_im, precision=highest
    )
    imag_part = jnp.einsum(form, left_re, right_im, precision=highest) + jnp.einsum(
        form, left_im, right_re, precision=highest
    )
    return (real_part, imag_part)


def couple_tops(spread, tr_part, list_source, list_kind, list_count):
    listed = list_source.shape[1]
    keep = (jnp.arange(listed)[None, :] < list_count[:, None]).astype(jnp.float32)
    gathered = jnp.take(spread, list_source, axis=2)
    factor = jnp.take(tr_part, list_kind, axis=1) * keep[None, :, :, None]
    out_re = jnp.sum(gathered[0] * factor[0] - gathered[1] * factor[1], axis=2)
    out_im = jnp.sum(gathered[0] * factor[1] + gathered[1] * factor[0], axis=2)
    return jnp.stack([out_re, out_im])


def local(
    current,
    near_block,
    neighbours,
    near_count,
    radiation,
    stencil,
    stencil_weight,
    child_shift,
    list_source,
    list_kind,
    list_count,
    translation,
):
    box_total = lax.axis_size("box")
    box_place = lax.axis_index("box")
    dir_place = lax.axis_index("dir")
    leaf_total = current.shape[1]
    slot_total = near_block.shape[2]
    own_width = near_block.shape[3]
    leaf_samples = radiation.shape[-1]
    padded = with_halo(current, (("box", 1),), leaf_total)
    local_index = neighbours - (box_place * leaf_total - leaf_total)
    picked = jnp.take(padded, local_index, axis=1)
    live = (jnp.arange(slot_total)[None, :] < near_count[:, None]).astype(jnp.float32)
    picked = picked * live[None, :, :, None]
    near_re, near_im = complex_apply(
        "bsuv,bsv->bu", near_block[0], near_block[1], picked[0], picked[1]
    )
    own_rows = lax.dynamic_slice_in_dim(current, dir_place * own_width, own_width, 2)
    part_re, part_im = complex_apply(
        "pbuk,bu->pbk", radiation[0], radiation[1], own_rows[0], own_rows[1]
    )
    share = stencil.shape[0]
    points = stencil.shape[1]
    parents = leaf_total // 8
    leaf_re, leaf_im = lax.psum((part_re, part_im), "dir")
    rimmed = jnp.stack([leaf_re, leaf_im])
    columns = jnp.arange(leaf_samples, dtype=jnp.int32)
    interp = jnp.zeros((share, leaf_samples), jnp.float32)
    for point in range(points):
        match = (stencil[:, point][:, None] == columns[None, :]).astype(jnp.float32)
        interp = interp + match * stencil_weight[:, point][:, None]
    shift_re, shift_im = (child_shift[0], child_shift[1])
    up_all = jnp.einsum("xpbk,qk->xpbq", rimmed, interp, precision=highest)
    up_all = up_all.reshape(2, up_all.shape[1], parents, 8, share)
    top_re = jnp.sum(up_all[0] * shift_re - up_all[1] * shift_im, axis=2)
    top_im = jnp.sum(up_all[0] * shift_im + up_all[1] * shift_re, axis=2)
    top = jnp.stack([top_re, top_im])
    piece = share // box_total
    tr_part = lax.dynamic_slice_in_dim(translation, box_place * piece, piece, 2)
    spread = lax.all_to_all(top, "box", split_axis=3, concat_axis=2, tiled=True)
    back = lax.all_to_all(
        couple_tops(spread, tr_part, list_source, list_kind, list_count),
        "box",
        split_axis=2,
        concat_axis=3,
        tiled=True,
    )
    back_re, back_im = (back[0], back[1])
    lower_re = back_re[:, :, None, :] * shift_re + back_im[:, :, None, :] * shift_im
    lower_im = back_im[:, :, None, :] * shift_re - back_re[:, :, None, :] * shift_im
    lowered = jnp.stack([lower_re, lower_im]).reshape(2, lower_re.shape[0], leaf_total, share)
    settled = jnp.einsum("xpbq,qk->xpbk", lowered, interp, precision=highest)
    income_re, income_im = lax.psum((settled[0], settled[1]), "dir")
    far_re = jnp.einsum("pbuk,pbk->bu", radiation[0], income_re, precision=highest) + jnp.einsum(
        "pbuk,pbk->bu", radiation[1], income_im, precision=highest
    )
    far_im = jnp.einsum("pbuk,pbk->bu", radiation[0], income_im, precision=highest) - jnp.einsum(
        "pbuk,pbk->bu", radiation[1], income_re, precision=highest
    )
    return jnp.stack([near_re + far_re, near_im + far_im])


def solution(mesh):
    return jax.shard_map(
        local,
        mesh=mesh,
        in_specs=(
            P(None, "box", None),
            P(None, "box", None, "dir", None),
            P("box", None),
            P("box"),
            P(None, None, "box", "dir", None),
            P("dir", None),
            P("dir", None),
            P(None, None, "dir"),
            P(),
            P(),
            P(),
            P(None, None, "dir"),
        ),
        out_specs=P(None, "box", "dir"),
        check_vma=False,
    )
```

profile of v0, /device:TPU:2, one launch (start us, length us, event | category | flops | bytes accessed | tf_op | source)
XLA Modules:
  0.0 378.7 jit_solution(5923571155313339202)
XLA Ops:
  7.3 1.9 collective-permute-start
  9.3 3.6 collective-permute-start.1
  12.9 1.7 slice_bitcast_fusion.3
  21.7 14.5 %gather_fusion.2 = f32[2048,2,4]{2,1,0:T(2,128)} fusion(f32[2,8,4]{2,0,1:T(2,128)S(1)} %copy.138, s32[2048]{0:T(1024)S(1)} %broadcast_clamp_fusion), kind=kCustom, calls=%fused_computation.2 | custom fusion | bytes 139264 | tf_op jit(solution)/shard_map/jit(_take)/gather | solution.py:36
  36.2 6.5 %multiply_bitcast_fusion = f32[2,128,16,4]{3,0,2,1:T(2,128)S(1)} fusion(f32[128,16,2,4]{3,2,1,0:T(2,128)} %bitcast.190, pred[128,16]{1,0:T(8,128)(4,1)S(1)} %copy.106, f32[128,16]{1,0:T(8,128)S(1)} %fusion.63), kind=kLoop, calls=%fused_computation.7 | loop fusion | flops 32768 | bytes 141312 | tf_op jit(solution)/shard_map/mul | solution.py:36
  42.7 2.6 fusion.79
  48.9 111.1 %all-reduce.7.cloned.1.call-done = (f32[1,2,32,512]{3,2,1,0:T(8,128)}, f32[1,2,32,512]{3,2,1,0:T(8,128)}) async-done(((f32[1,2,32,512]{3,2,1,0:T(8,128)}, f32[1,2,32,512]{3,2,1,0:T(8,128)}), (f32[1,2,32,512]{3,2,1,0:T(8,128)}, f32[1,2,32,512]{3,2,1,0:T(8,128)})) %all-reduce.7.cloned.1.call-update) | async-done | bytes 262160 | tf_op jit(solution)/shard_map/psum | solution.py:78
  162.5 7.4 %all-to-all-start = ((f32[2,2,4,128]{2,1,0,3:T(2,128)}), f32[2,2,4,128]{2,1,0,3:T(2,128)S(1)}, u32[]{:S(2)}, u32[]{:S(2)}) async-start(f32[2,2,4,128]{2,1,0,3:T(2,128)} %copy.100), calls=%async_computation | async-start | bytes 524288 | tf_op jit(solution)/shard_map/all_to_all | solution.py:93
  169.9 2.6 fusion.19
  172.5 5.1 %all-to-all-done = f32[2,2,4,128]{2,1,0,3:T(2,128)S(1)} async-done(((f32[2,2,4,128]{2,1,0,3:T(2,128)}), f32[2,2,4,128]{2,1,0,3:T(2,128)S(1)}, u32[]{:S(2)}, u32[]{:S(2)}) %all-to-all-start) | async-done | bytes 8224 | tf_op jit(solution)/shard_map/all_to_all | solution.py:93
  178.4 1.8 copy.136
  180.2 17.9 %gather_fusion.1 = f32[2048,2,2,4]{3,2,1,0:T(2,128)} fusion(f32[2,2,128,4]{3,1,2,0:T(2,128)S(1)} %bitcast.188, s32[2048]{0:T(1024)S(1)} %broadcast_clamp_fusion.1), kind=kCustom, calls=%fused_computation.1 | custom fusion | bytes 270336 | tf_op jit(solution)/shard_map/jit(_take)/gather | solution.py:35
  198.1 9.6 %fusion = f32[2,2,128,16,4]{4,1,3,2,0:T(2,128)S(1)} fusion(f32[128,16,2,2,4]{4,3,2,1,0:T(2,128)} %bitcast.189, pred[128,16]{1,0:T(8,128)(4,1)S(1)} %copy.99), kind=kLoop, calls=%fused_computation.4 | loop fusion | flops 32768 | bytes 264192 | tf_op jit(solution)/shard_map/jit(_take)/select_n | solution.py:35
  207.7 4.5 %subtract_reduce_fusion = (f32[2,128,4]{2,0,1:T(2,128)S(1)}, f32[2,128,4]{2,0,1:T(2,128)S(1)}) fusion(f32[2,2,128,16,4]{4,1,3,2,0:T(2,128)S(1)} %fusion, f32[128,16,4]{2,1,0:T(8,128)S(1)} %bitcast.192, f32[128,16,4]{2,1,0:T(8,128)S(1)} %bitcast.191), kind=kLoop, calls=%fused_computation.9 | loop fusion | flops 129024 | bytes 204800 | tf_op jit(solution)/shard_map/reduce_sum | solution.py:37
  213.3 5.0 %all-to-all-start.1 = ((f32[2,2,128,4]{3,1,0,2:T(2,128)}), f32[2,2,128,4]{3,1,0,2:T(2,128)S(1)}, u32[]{:S(2)}, u32[]{:S(2)}) async-start(f32[2,2,128,4]{3,1,0,2:T(2,128)} %copy.109), calls=%async_computation.1 | async-start | bytes 524288 | tf_op jit(solution)/shard_map/all_to_all | solution.py:94
  218.3 2.7 fusion.21
  221.0 5.1 %all-to-all-done.1 = f32[2,2,128,4]{3,1,0,2:T(2,128)S(1)} async-done(((f32[2,2,128,4]{3,1,0,2:T(2,128)}), f32[2,2,128,4]{3,1,0,2:T(2,128)S(1)}, u32[]{:S(2)}, u32[]{:S(2)}) %all-to-all-start.1) | async-done | bytes 8224 | tf_op jit(solution)/shard_map/all_to_all | solution.py:94
  229.9 2.7 fusion.23
  232.8 2.7 fusion.17
  235.5 124.6 %all-reduce.5.cloned.1.call-done = (f32[2,32,512]{2,1,0:T(8,128)}, f32[2,32,512]{2,1,0:T(8,128)}) async-done(((f32[2,32,512]{2,1,0:T(8,128)}, f32[2,32,512]{2,1,0:T(8,128)}), (f32[2,32,512]{2,1,0:T(8,128)}, f32[2,32,512]{2,1,0:T(8,128)})) %all-reduce.5.cloned.1.call-update) | async-done | bytes 262160 | tf_op jit(solution)/shard_map/psum | solution.py:106
  360.1 3.2 fusion.3
  363.3 3.2 fusion.9
  366.4 2.3 fusion.11
  368.7 2.3 fusion.1
  (124 shorter events, 20.3 us)
Async XLA Ops:
  6.5 14.7 %copy-start = (f32[2,8,128]{2,1,0:T(8,128)S(1)}, f32[2,8,128]{2,1,0:T(8,128)}, u32[]{:S(2)}) copy-start(f32[2,8,128]{2,1,0:T(8,128)} %param.23) | copy-start | bytes 24580
  6.5 153.4 %all-reduce.7.cloned.1.call-start = ((), (), s32[]{:S(2)}) async-start(), calls=%async_computation.3 | async-start | bytes 524288 | tf_op jit(solution)/shard_map/psum | solution.py:78
  7.3 39.2 %collective-permute-start = (f32[2,32,128]{2,0,1:T(2,128)S(1)}, f32[2,32,128]{2,0,1:T(2,128)S(1)}, u32[]{:S(2)}, u32[]{:S(2)}) collective-permute-start(f32[2,32,128]{2,0,1:T(2,128)S(1)} %copy.93), channel_id=1, source_target_pairs={{0,16},{16,32},{32,48},{48,64},{64,80},{80,96},{96,112},{112,128},... | collective-permute-start | bytes 98312 | tf_op jit(solution)/shard_map/ppermute | solution.py:14
  9.3 37.2 %collective-permute-start.1 = (f32[2,32,128]{2,0,1:T(2,128)S(1)}, f32[2,32,128]{2,0,1:T(2,128)S(1)}, u32[]{:S(2)}, u32[]{:S(2)}) collective-permute-start(f32[2,32,128]{2,0,1:T(2,128)S(1)} %copy.93), channel_id=1, source_target_pairs={{16,0},{32,16},{48,32},{64,48},{80,64},{96,80},{112,96},{128,112},... | collective-permute-start | bytes 98312 | tf_op jit(solution)/shard_map/ppermute | solution.py:17
  21.0 24.6 %copy-start.7 = (f32[8,128]{1,0:T(8,128)}, f32[8,128]{1,0:T(8,128)S(1)}, u32[]{:S(2)}) copy-start(f32[8,128]{1,0:T(8,128)S(1)} %get-tuple-element.29) | copy-start | bytes 12292
  21.0 24.6 %copy-start.9 = (f32[8,128]{1,0:T(8,128)}, f32[8,128]{1,0:T(8,128)S(1)}, u32[]{:S(2)}) copy-start(f32[8,128]{1,0:T(8,128)S(1)} %get-tuple-element.30) | copy-start | bytes 12292
  48.0 113.5 %copy-start.8 = (f32[8,128]{1,0:T(8,128)S(1)}, f32[8,128]{1,0:T(8,128)}, u32[]{:S(2)}) copy-start(f32[8,128]{1,0:T(8,128)} %copy-done.7) | copy-start | bytes 12292
  48.0 113.5 %copy-start.10 = (f32[8,128]{1,0:T(8,128)S(1)}, f32[8,128]{1,0:T(8,128)}, u32[]{:S(2)}) copy-start(f32[8,128]{1,0:T(8,128)} %copy-done.9) | copy-start | bytes 12292
  162.5 15.1 %all-to-all-start = ((f32[2,2,4,128]{2,1,0,3:T(2,128)}), f32[2,2,4,128]{2,1,0,3:T(2,128)S(1)}, u32[]{:S(2)}, u32[]{:S(2)}) async-start(f32[2,2,4,128]{2,1,0,3:T(2,128)} %copy.100), calls=%async_computation | async-start | bytes 524288 | tf_op jit(solution)/shard_map/all_to_all | solution.py:93
  198.1 9.6 %copy-start.1 = (f32[1,128,16,4]{3,0,2,1:T(1,128)S(1)}, f32[1,128,16,4]{3,0,2,1:T(1,128)}, u32[]{:S(2)}) copy-start(f32[1,128,16,4]{3,0,2,1:T(1,128)} %get-tuple-element.16) | copy-start | bytes 98308
  207.7 10.6 %copy-start.2 = (f32[32,6,128,1]{2,0,1,3:T(8,128)S(1)}, f32[32,6,128,1]{2,0,1,3:T(8,128)}, u32[]{:S(2)}) copy-start(f32[32,6,128,1]{2,0,1,3:T(8,128)} %get-tuple-element.43) | copy-start | bytes 294916
  212.2 16.2 %copy-start.5 = (f32[32,128]{1,0:T(8,128)S(1)}, f32[32,128]{1,0:T(8,128)}, u32[]{:S(2)}) copy-start(f32[32,128]{1,0:T(8,128)} %get-tuple-element.41) | copy-start | bytes 49156
  212.2 16.2 %copy-start.6 = (f32[32,128]{1,0:T(8,128)S(1)}, f32[32,128]{1,0:T(8,128)}, u32[]{:S(2)}) copy-start(f32[32,128]{1,0:T(8,128)} %get-tuple-element.42) | copy-start | bytes 49156
  212.2 16.3 %copy-start.19 = (s32[128]{0:T(128)S(1)}, s32[128]{0:T(128)}, u32[]{:S(2)}) copy-start(s32[128]{0:T(128)} %get-tuple-element.31) | copy-start | bytes 1540
  212.2 16.3 %copy-start.20 = (s32[128]{0:T(128)S(1)}, s32[128]{0:T(128)}, u32[]{:S(2)}) copy-start(s32[128]{0:T(128)} %get-tuple-element.32) | copy-start | bytes 1540
  212.3 16.3 %copy-start.21 = (s32[128]{0:T(128)S(1)}, s32[128]{0:T(128)}, u32[]{:S(2)}) copy-start(s32[128]{0:T(128)} %get-tuple-element.33) | copy-start | bytes 1540
  212.3 16.3 %copy-start.22 = (s32[128]{0:T(128)S(1)}, s32[128]{0:T(128)}, u32[]{:S(2)}) copy-start(s32[128]{0:T(128)} %get-tuple-element.34) | copy-start | bytes 1540
  212.3 16.3 %copy-start.23 = (f32[128]{0:T(128)S(1)}, f32[128]{0:T(128)}, u32[]{:S(2)}) copy-start(f32[128]{0:T(128)} %get-tuple-element.35) | copy-start | bytes 1540
  212.3 16.3 %copy-start.24 = (f32[128]{0:T(128)S(1)}, f32[128]{0:T(128)}, u32[]{:S(2)}) copy-start(f32[128]{0:T(128)} %get-tuple-element.36) | copy-start | bytes 1540
  212.3 16.3 %copy-start.25 = (f32[128]{0:T(128)S(1)}, f32[128]{0:T(128)}, u32[]{:S(2)}) copy-start(f32[128]{0:T(128)} %get-tuple-element.37) | copy-start | bytes 1540
  212.3 16.3 %copy-start.26 = (f32[128]{0:T(128)S(1)}, f32[128]{0:T(128)}, u32[]{:S(2)}) copy-start(f32[128]{0:T(128)} %get-tuple-element.38) | copy-start | bytes 1540
  213.3 12.8 %all-to-all-start.1 = ((f32[2,2,128,4]{3,1,0,2:T(2,128)}), f32[2,2,128,4]{3,1,0,2:T(2,128)S(1)}, u32[]{:S(2)}, u32[]{:S(2)}) async-start(f32[2,2,128,4]{3,1,0,2:T(2,128)} %copy.109), calls=%async_computation.1 | async-start | bytes 524288 | tf_op jit(solution)/shard_map/all_to_all | solution.py:94
  218.2 141.8 %all-reduce.5.cloned.1.call-start = ((), (), s32[]{:S(2)}) async-start(), calls=%async_computation.2 | async-start | bytes 524288 | tf_op jit(solution)/shard_map/psum | solution.py:106
  360.1 6.4 %copy-start.3 = (f32[2,32,512]{2,1,0:T(8,128)S(1)}, f32[2,32,512]{2,1,0:T(8,128)}, u32[]{:S(2)}) copy-start(f32[2,32,512]{2,1,0:T(8,128)} %get-tuple-element.9) | copy-start | bytes 393220
  (9 other events, 33.6 us)
Sparse Core Ops, SparseCore 0:
  19.8 140.1 all-reduce.6
  230.0 130.0 all-reduce.4
where the time goes:
time: 380 us; the launch traced here: 379 us
  waiting for transfers between devices  246 us (65%)
  local copies, waits for them, and re-layouts  50.1 us (13%)
  matrix products  27.6 us (7%)
  other arithmetic  23.1 us (6%)
  starting transfers between devices  18 us (5%)
  between operations  14 us (4%)
    psum x1, waiting for transfers between devices, local(): income_re, income_im = lax.psum((settled[0], settled[1]), 'dir')  125 us
    psum x1, waiting for transfers between devices, local(): leaf_re, leaf_im = lax.psum((part_re, part_im), 'dir')  111 us
    gather x1, local copies, waits for them, and re-layouts, couple_tops(): gathered = jnp.take(spread, list_source, axis=2)  17.9 us
    gather x1, local copies, waits for them, and re-layouts, couple_tops(): factor = jnp.take(tr_part, list_kind, axis=1) * keep[None, :, :, None]  14.5 us
    select_n x2, other arithmetic, couple_tops(): gathered = jnp.take(spread, list_source, axis=2)  9.6 us
  transfers between devices with their start and end apart: 6, of which 4 were waited for; matrix products, arithmetic and copies ran while one was open for 12% of the time, Pallas kernels for 0%

commit v1 on v0

v1 whole, which is shorter than its diff:
```python
import functools

import jax
import jax.numpy as jnp
from jax import lax
from jax.experimental import pallas as pl
from jax.experimental.pallas import tpu as pltpu
from jax.sharding import PartitionSpec as P

highest = lax.Precision.HIGHEST
f32 = jnp.float32
below, above = 1, 2
lead = 8
VMEM = pl.BlockSpec(memory_space=pltpu.VMEM)
SMEM = pl.BlockSpec(memory_space=pltpu.SMEM)
ANY = pl.BlockSpec(memory_space=pl.ANY)
params = pltpu.CompilerParams(vmem_limit_bytes=12 * 2**20)


def leaf_kernel(cuts, shares, current, stencil, weight, radiation, out, interp, patterns, columns, rows, samples, sems):
    pols, boxes, own, width = radiation.shape[1:]
    place = lax.axis_index("dir")
    step = boxes // cuts
    copies = []
    for cut in range(cuts):
        part = pl.ds(cut * step, step)
        copy = pltpu.make_async_copy(radiation.at[:, :, part], patterns.at[:, :, part], sems.at[cut])
        copy.start()
        copies.append(copy)
    piece = width // shares
    lanes = stencil.shape[1]
    row = lax.broadcasted_iota(jnp.int32, (128, lanes), 0)
    table = jnp.zeros((128, lanes), f32)
    for point in range(stencil.shape[0]):
        at = lax.rem(stencil[point : point + 1, :] - (place * piece - below) + width, width)
        table = table + jnp.where(row == at, weight[point : point + 1, :], 0.0)
    interp[...] = table
    for part in range(2):
        columns[part] = current[part].T
    mine = pl.ds(pl.multiple_of(place * own, own), own)
    real, imag = columns[0, mine, :], columns[1, mine, :]
    for cut in range(cuts):
        copies[cut].wait()
        for box in range(cut * step, (cut + 1) * step):
            cur_re, cur_im = real[:, box : box + 1], imag[:, box : box + 1]
            for pol in range(pols):
                rad_re, rad_im = patterns[0, pol, box], patterns[1, pol, box]
                at = pol * boxes + box
                rows[at : at + 1, :] = jnp.sum(rad_re * cur_re - rad_im * cur_im, axis=0, keepdims=True)
                at = (pols + pol) * boxes + box
                rows[at : at + 1, :] = jnp.sum(rad_re * cur_im + rad_im * cur_re, axis=0, keepdims=True)
    for block in range(width // 128):
        samples[lead + block * 128 : lead + block * 128 + 128, :] = rows[:, block * 128 : block * 128 + 128].T
    samples[lead - below : lead, :] = samples[lead + width - below : lead + width, :]
    samples[lead + width : lead + width + above, :] = samples[lead : lead + above, :]
    span = piece + below + above
    for share in range(shares):
        first = lead - below + share * piece
        out[share * span : (share + 1) * span, :] = samples[first : first + span, :]


def lift_kernel(shares, copies, received, interp, shift, out, total, tops):
    span = received.shape[0] // shares
    total[...] = jnp.zeros_like(total)
    part = received[0:span, :]
    for share in range(1, shares):
        part = part + received[share * span : (share + 1) * span, :]
    total[0:span, :] = part
    up = jnp.dot(total[...].T, interp[...], precision=highest, preferred_element_type=f32)
    shift_re, shift_im = shift[0], shift[1]
    half = up.shape[0] // 2
    lines = half // 8
    for line in range(lines):
        up_re, up_im = up[line * 8 : line * 8 + 8], up[half + line * 8 : half + line * 8 + 8]
        tops[line : line + 1, :] = jnp.sum(up_re * shift_re - up_im * shift_im, axis=0, keepdims=True)
        tops[lines + line : lines + line + 1, :] = jnp.sum(up_re * shift_im + up_im * shift_re, axis=0, keepdims=True)
    value = tops[...]
    for copy in range(copies):
        out[copy * 2 * lines : (copy + 1) * 2 * lines, :] = value


def lower_kernel(shares, span, parents, source, kind, count, received, translation, interp, shift, out, factors, down):
    kinds = translation.shape[1]
    lines = down.shape[0] // 16
    pols = lines // parents
    first = lax.axis_index("box") * parents
    factors[...] = jnp.zeros_like(factors)
    factors[:, 0:kinds, :] = translation[...]
    shift_re, shift_im = shift[0], shift[1]
    for parent in range(parents):
        used = count[first + parent]
        by_re = jnp.zeros((2 * pols, 128), f32)
        by_im = jnp.zeros((2 * pols, 128), f32)
        for slot in range(source.shape[0]):
            origin = source[slot, first + parent]
            which = jnp.where(slot < used, kind[slot, first + parent], kinds)
            begin = (origin // parents) * (2 * lines) + lax.rem(origin, parents)
            tops = received[pl.ds(begin, 2 * pols, stride=parents), :]
            by_re = by_re + tops * factors[0, pl.ds(which, 1), :]
            by_im = by_im + tops * factors[1, pl.ds(which, 1), :]
        moved_re = by_re[0:pols] - by_im[pols:]
        moved_im = by_im[0:pols] + by_re[pols:]
        for pol in range(pols):
            mine_re, mine_im = moved_re[pol : pol + 1], moved_im[pol : pol + 1]
            at = (pol * parents + parent) * 8
            down[at : at + 8, :] = mine_re * shift_re + mine_im * shift_im
            down[lines * 8 + at : lines * 8 + at + 8, :] = mine_im * shift_re - mine_re * shift_im
    settled = lax.dot_general(
        interp[0:40, :], down[...], (((1,), (1,)), ((), ())), precision=highest, preferred_element_type=f32
    )
    value = settled[0:span]
    for share in range(shares):
        out[share * span : (share + 1) * span, :] = value


def near_kernel(neighbours, near_count, low, current, high, blocks, out, padded):
    slots, boxes = neighbours.shape
    first = lax.axis_index("box") * boxes - boxes
    for part in range(2):
        padded[part, 0:boxes, :] = low[part]
        padded[part, boxes : 2 * boxes, :] = current[part]
        padded[part, 2 * boxes : 3 * boxes, :] = high[part]
        padded[part, 3 * boxes :, :] = jnp.zeros((8, 128), f32)
    for box in range(boxes):
        used = near_count[box]
        sum_re = jnp.zeros(out.shape[2:], f32)
        sum_im = jnp.zeros(out.shape[2:], f32)
        for slot in range(slots):
            at = jnp.where(slot < used, neighbours[slot, box] - first, 3 * boxes)
            cur_re, cur_im = padded[0, pl.ds(at, 1), :], padded[1, pl.ds(at, 1), :]
            block_re, block_im = blocks[0, box, slot], blocks[1, box, slot]
            sum_re = sum_re + (block_re * cur_re - block_im * cur_im)
            sum_im = sum_im + (block_re * cur_im + block_im * cur_re)
        out[0, box] = sum_re
        out[1, box] = sum_im


def field_kernel(shares, received, radiation, near, out, samples, rows):
    pols, boxes, own, width = radiation.shape[1:]
    span = received.shape[0] // shares
    piece = width // shares
    samples[...] = jnp.zeros_like(samples)
    for share in range(shares):
        first = lead - below + share * piece
        samples[first : first + span, :] += received[share * span : (share + 1) * span, :]
    samples[lead + width - below : lead + width, :] += samples[lead - below : lead, :]
    samples[lead : lead + above, :] += samples[lead + width : lead + width + above, :]
    for block in range(width // 128):
        rows[:, block * 128 : block * 128 + 128] = samples[lead + block * 128 : lead + block * 128 + 128, :].T
    lane = lax.broadcasted_iota(jnp.int32, (own, boxes), 1)
    all_re = jnp.zeros((own, boxes), f32)
    all_im = jnp.zeros((own, boxes), f32)
    for box in range(boxes):
        sum_re, sum_im = near[0, box], near[1, box]
        for pol in range(pols):
            at_re, at_im = pol * boxes + box, (pols + pol) * boxes + box
            for block in range(width // 128):
                cut = slice(block * 128, block * 128 + 128)
                in_re, in_im = rows[at_re : at_re + 1, cut], rows[at_im : at_im + 1, cut]
                rad_re, rad_im = radiation[0, pol, box, :, cut], radiation[1, pol, box, :, cut]
                sum_re = sum_re + (rad_re * in_re + rad_im * in_im)
                sum_im = sum_im + (rad_re * in_im - rad_im * in_re)
        all_re = jnp.where(lane == box, jnp.sum(sum_re, axis=1, keepdims=True), all_re)
        all_im = jnp.where(lane == box, jnp.sum(sum_im, axis=1, keepdims=True), all_im)
    out[0] = all_re
    out[1] = all_im


def local(
    current,
    near_block,
    neighbours,
    near_count,
    radiation,
    stencil,
    stencil_weight,
    child_shift,
    list_source,
    list_kind,
    list_count,
    translation,
):
    box_total, dir_total = lax.axis_size("box"), lax.axis_size("dir")
    _, pols, boxes, own, width = radiation.shape
    share = stencil.shape[0]
    parents = boxes // 8
    piece = width // dir_total
    span = piece + below + above
    lanes = 2 * pols * boxes
    held = lead + width + 8
    cuts = 4
    shape = functools.partial(jax.ShapeDtypeStruct, dtype=f32)

    forward = [(i, i + 1) for i in range(box_total - 1)]
    low = lax.ppermute(current, "box", forward)
    high = lax.ppermute(current, "box", [(b, a) for a, b in forward])

    windows, interp = pl.pallas_call(
        functools.partial(leaf_kernel, cuts, dir_total),
        out_shape=(shape((dir_total * span, lanes)), shape((128, share))),
        in_specs=[VMEM, VMEM, VMEM, ANY],
        out_specs=(VMEM, VMEM),
        scratch_shapes=[
            pltpu.VMEM(radiation.shape, f32),
            pltpu.VMEM((2, current.shape[2], boxes), f32),
            pltpu.VMEM((lanes, width), f32),
            pltpu.VMEM((held, lanes), f32),
            pltpu.SemaphoreType.DMA((cuts,)),
        ],
        compiler_params=params,
        name="leaf",
    )(current, stencil.T, stencil_weight.T, radiation)
    windows = lax.all_to_all(windows.reshape(dir_total, 1, span * lanes), "dir", 0, 0, tiled=True)

    tops = pl.pallas_call(
        functools.partial(lift_kernel, dir_total, box_total),
        out_shape=shape((box_total * lanes // 8, share)),
        in_specs=[VMEM] * 3,
        out_specs=VMEM,
        scratch_shapes=[pltpu.VMEM((128, lanes), f32), pltpu.VMEM((lanes // 8, share), f32)],
        compiler_params=params,
        name="lift",
    )(windows.reshape(dir_total * span, lanes), interp, child_shift)
    tops = lax.all_to_all(tops.reshape(box_total, 1, lanes // 8 * share), "box", 0, 0, tiled=True)

    near = pl.pallas_call(
        near_kernel,
        out_shape=shape((2, boxes, own, 128)),
        in_specs=[SMEM, SMEM] + [VMEM] * 4,
        out_specs=VMEM,
        scratch_shapes=[pltpu.VMEM((2, 3 * boxes + 8, 128), f32)],
        compiler_params=params,
        name="near",
    )(neighbours.T, near_count, low, current, high, near_block)

    income = pl.pallas_call(
        functools.partial(lower_kernel, dir_total, span, parents),
        out_shape=shape((dir_total * span, lanes)),
        in_specs=[SMEM] * 3 + [VMEM] * 4,
        out_specs=VMEM,
        scratch_shapes=[pltpu.VMEM((2, 16, share), f32), pltpu.VMEM((lanes, share), f32)],
        compiler_params=params,
        name="lower",
    )(list_source.T, list_kind.T, list_count, tops.reshape(-1, share), translation, interp, child_shift)
    income = lax.all_to_all(income.reshape(dir_total, 1, span * lanes), "dir", 0, 0, tiled=True)

    field = pl.pallas_call(
        functools.partial(field_kernel, dir_total),
        out_shape=shape((2, own, boxes)),
        in_specs=[VMEM] * 3,
        out_specs=VMEM,
        scratch_shapes=[pltpu.VMEM((held, lanes), f32), pltpu.VMEM((lanes, width), f32)],
        compiler_params=params,
        name="field",
    )(income.reshape(dir_total * span, lanes), radiation, near)
    return field.transpose(0, 2, 1)


def solution(mesh):
    return jax.shard_map(
        local,
        mesh=mesh,
        in_specs=(
            P(None, "box", None),
            P(None, "box", None, "dir", None),
            P("box", None),
            P("box"),
            P(None, None, "box", "dir", None),
            P("dir", None),
            P("dir", None),
            P(None, None, "dir"),
            P(),
            P(),
            P(),
            P(None, None, "dir"),
        ),
        out_specs=P(None, "box", "dir"),
        check_vma=False,
    )
```

time: 380 us -> 84.8 us (0.22)
  the two profiles are of different devices: /device:TPU:2 before, /device:TPU:32 now
where the time goes in v1:
time: 84.8 us; the launch traced here: 84.4 us
  blocking collectives  49.7 us (59%)
  waiting for transfers between devices  13.8 us (16%)
  starting transfers between devices  9.63 us (11%)
  Pallas kernels  6.03 us (7%)
  local copies, waits for them, and re-layouts  5.17 us (6%)
    all_to_all x1, blocking collectives, local(): lax.all_to_all(windows.reshape(dir_total, 1, span * lanes), 'dir', 0, 0,...  33.5 us
    all_to_all x1, blocking collectives, local(): lax.all_to_all(tops.reshape(box_total, 1, lanes // 8 * share), 'box', 0,...  16.2 us
    all_to_all x1, waiting for transfers between devices, local(): lax.all_to_all(income.reshape(dir_total, 1, span * lanes), 'dir', 0, 0, t...  11.5 us
    all_to_all x1, starting transfers between devices, local(): lax.all_to_all(income.reshape(dir_total, 1, span * lanes), 'dir', 0, 0, t...  6.72 us
    unnamed x28, local copies, waits for them, and re-layouts  5.17 us
    ppermute x1, waiting for transfers between devices, local(): high = lax.ppermute(current, 'box', [(b, a) for a, b in forward])  2.28 us
    pallas_call x1, Pallas kernels, local(): pl.pallas_call(functools.partial(lower_kernel, dir_total, span, parents),...  2.23 us
  transfers between devices with their start and end apart: 3, of which 2 were waited for; matrix products, arithmetic and copies ran while one was open for 0% of the time, Pallas kernels for 1%

profile of v1, /device:TPU:32, one launch (start us, length us, event | category | flops | bytes accessed | tf_op | source)
XLA Modules:
  0.0 84.4 jit_solution(12821571828285576409)
XLA Ops:
  0.0 1.6 %copy-done = f32[2,2,32,8,512]{4,3,2,1,0:T(8,128)S(1)} copy-done((f32[2,2,32,8,512]{4,3,2,1,0:T(8,128)S(1)}, f32[2,2,32,8,512]{4,3,2,1,0:T(8,128)}, u32[]{:S(2)}) %copy-start) | copy-done | bytes 2097176
  1.6 0.8 copy-done.3
  2.4 0.7 copy-done.10
  3.1 0.7 copy-done.11
  3.7 0.0 copy-start.4
  3.8 0.0 copy-start.9
  3.8 0.0 copy-start.12
  3.8 1.5 %leaf.1 = (f32[560,128]{1,0:T(8,128)S(1)}, f32[128,128]{1,0:T(8,128)S(1)}) custom-call(f32[2,32,128]{2,1,0:T(8,128)S(1)} %copy-done.3, s32[4,128]{1,0:T(4,128)S(1)} %bitcast.20, f32[4,128]{1,0:T(4,128)S(1)} %bitcast.21, f32[2,2,32,8,512]{4,3,2,1,0:T(8,128)S(1)} %copy-done), custom_call_target="tpu_custom_call" | custom-call | tf_op jit(solution)/shard_map/leaf/pallas_call | solution.py:198
  5.2 33.5 %all_to_all.15 = f32[16,1,4480]{2,1,0:T(1,128)S(1)} all-to-all(f32[16,1,4480]{2,1,0:T(1,128)S(1)} %bitcast.16), channel_id=1, replica_groups=mesh['box'=32,'dir'=16] {'dir'}, dimensions={0} | all-to-all | bytes 573440 | tf_op jit(solution)/shard_map/all_to_all | solution.py:213
  38.7 0.0 copy-done.5
  38.7 0.3 lift.1
  39.1 16.2 %all_to_all.16 = f32[32,1,2048]{2,1,0:T(1,128)S(1)} all-to-all(f32[32,1,2048]{2,1,0:T(1,128)S(1)} %bitcast.15), channel_id=1, replica_groups=mesh['box'=32,'dir'=16] {'box'}, dimensions={0} | all-to-all | bytes 524288 | tf_op jit(solution)/shard_map/all_to_all | solution.py:224
  55.2 0.0 copy-done.6
  55.2 2.2 %lower.1 = f32[560,128]{1,0:T(8,128)} custom-call(s32[16,128]{1,0:T(8,128)S(1)} %bitcast.17, s32[16,128]{1,0:T(8,128)S(1)} %bitcast.18, s32[128]{0:T(128)S(1)} %copy-done.13, f32[512,128]{1,0:T(8,128)S(1)} %bitcast.14, f32[2,8,128]{2,1,0:T(8,128)S(1)} %copy-done.8, f32[128,128]{1,0:T(8,128)S(1)} %get-tuple-element.8.interp, f32[2,8,128]{2,1,0:T(8,128)S(1)} %copy-done.5), custom_call_target="tpu_custom_call" | custom-call | tf_op jit(solution)/shard_map/lower/pallas_call | solution.py:236
  57.5 6.7 %all-to-all-start.2 = ((f32[16,1,4480]{2,1,0:T(1,128)}), f32[16,1,4480]{2,1,0:T(1,128)S(1)}, u32[]{:S(2)}, u32[]{:S(2)}) async-start(f32[16,1,4480]{2,1,0:T(1,128)} %bitcast.8), calls=%async_computation.2 | async-start | bytes 573440 | tf_op jit(solution)/shard_map/all_to_all | solution.py:245
  64.2 1.6 %collective-permute-start = (f32[2,32,128]{2,1,0:T(8,128)S(1)}, f32[2,32,128]{2,1,0:T(8,128)S(1)}, u32[]{:S(2)}, u32[]{:S(2)}) collective-permute-start(f32[2,32,128]{2,1,0:T(8,128)S(1)} %copy-done.4), channel_id=1, source_target_pairs={{0,16},{16,32},{32,48},{48,64},{64,80},{80,96},{96,112},{112,128},... | collective-permute-start | bytes 98312 | tf_op jit(solution)/shard_map/ppermute | solution.py:195
  65.8 1.3 %collective-permute-start.1 = (f32[2,32,128]{2,1,0:T(8,128)S(1)}, f32[2,32,128]{2,1,0:T(8,128)S(1)}, u32[]{:S(2)}, u32[]{:S(2)}) collective-permute-start(f32[2,32,128]{2,1,0:T(8,128)S(1)} %copy-done.4), channel_id=1, source_target_pairs={{16,0},{32,16},{48,32},{64,48},{80,64},{96,80},{112,96},{128,112},... | collective-permute-start | bytes 98312 | tf_op jit(solution)/shard_map/ppermute | solution.py:196
  67.1 0.0 collective-permute-done.low
  67.1 2.3 %collective-permute-done.1.high = f32[2,32,128]{2,1,0:T(8,128)S(1)} collective-permute-done((f32[2,32,128]{2,1,0:T(8,128)S(1)}, f32[2,32,128]{2,1,0:T(8,128)S(1)}, u32[]{:S(2)}, u32[]{:S(2)}) %collective-permute-start.1) | collective-permute-done | bytes 32800 | tf_op jit(solution)/shard_map/ppermute | solution.py:196
  69.4 0.0 copy-done.9
  69.4 1.4 %copy-done.2 = f32[2,32,6,8,128]{4,3,2,1,0:T(8,128)S(1)} copy-done((f32[2,32,6,8,128]{4,3,2,1,0:T(8,128)S(1)}, f32[2,32,6,8,128]{4,3,2,1,0:T(8,128)}, u32[]{:S(2)}) %copy-start.2) | copy-done | bytes 1572888
  70.8 0.9 %near.1 = f32[2,32,8,128]{3,2,1,0:T(8,128)S(1)} custom-call(s32[6,32]{1,0:T(8,128)S(1)} %bitcast.19, s32[32]{0:T(128)S(1)} %copy-done.12, f32[2,32,128]{2,1,0:T(8,128)S(1)} %collective-permute-done.low, f32[2,32,128]{2,1,0:T(8,128)S(1)} %copy-done.4, f32[2,32,128]{2,1,0:T(8,128)S(1)} %collective-permute-done.1.high, f32[2,32,6,8,128]{4,3,2,1,0:T(8,128)S(1)} %copy-done.2), custom_call_target="tpu_custom_call" | custom-call | tf_op jit(solution)/shard_map/near/pallas_call | solution.py:226
  71.7 11.5 %all-to-all-done.2 = f32[16,1,4480]{2,1,0:T(1,128)S(1)} async-done(((f32[16,1,4480]{2,1,0:T(1,128)}), f32[16,1,4480]{2,1,0:T(1,128)S(1)}, u32[]{:S(2)}, u32[]{:S(2)}) %all-to-all-start.2) | async-done | bytes 286752 | tf_op jit(solution)/shard_map/all_to_all | solution.py:245
  83.2 1.1 %field.1 = f32[2,8,32]{2,1,0:T(8,128)} custom-call(f32[560,128]{1,0:T(8,128)S(1)} %bitcast.13, f32[2,2,32,8,512]{4,3,2,1,0:T(8,128)S(1)} %copy-done.1, f32[2,32,8,128]{3,2,1,0:T(8,128)S(1)} %near.1), custom_call_target="tpu_custom_call" | custom-call | tf_op jit(solution)/shard_map/field/pallas_call | solution.py:247
  (17 shorter events, 0.0 us)
Async XLA Ops:
  0.0 55.2 %copy-start.13 = (s32[128]{0:T(128)S(1)}, s32[128]{0:T(128)}, u32[]{:S(2)}) copy-start(s32[128]{0:T(128)} %count.1) | copy-start | bytes 1540
  0.0 1.6 %copy-start = (f32[2,2,32,8,512]{4,3,2,1,0:T(8,128)S(1)}, f32[2,2,32,8,512]{4,3,2,1,0:T(8,128)}, u32[]{:S(2)}) copy-start(f32[2,2,32,8,512]{4,3,2,1,0:T(8,128)} %radiation.3) | copy-start | bytes 6291460
  1.6 0.8 copy-start.3
  2.4 0.7 copy-start.10
  3.0 0.7 copy-start.11
  3.7 35.0 %copy-start.5 = (f32[2,8,128]{2,1,0:T(8,128)S(1)}, f32[2,8,128]{2,1,0:T(8,128)}, u32[]{:S(2)}) copy-start(f32[2,8,128]{2,1,0:T(8,128)} %shift.3) | copy-start | bytes 24580
  3.7 51.5 %copy-start.6 = (s32[128,16]{0,1:T(8,128)S(1)}, s32[128,16]{0,1:T(8,128)}, u32[]{:S(2)}) copy-start(s32[128,16]{0,1:T(8,128)} %param.20) | copy-start | bytes 24580
  3.7 51.5 %copy-start.7 = (s32[128,16]{0,1:T(8,128)S(1)}, s32[128,16]{0,1:T(8,128)}, u32[]{:S(2)}) copy-start(s32[128,16]{0,1:T(8,128)} %param.21) | copy-start | bytes 24580
  3.7 51.5 %copy-start.8 = (f32[2,8,128]{2,1,0:T(8,128)S(1)}, f32[2,8,128]{2,1,0:T(8,128)}, u32[]{:S(2)}) copy-start(f32[2,8,128]{2,1,0:T(8,128)} %translation.1) | copy-start | bytes 24580
  3.7 60.4 %copy-start.4 = (f32[2,32,128]{2,1,0:T(8,128)S(1)}, f32[2,32,128]{2,1,0:T(8,128)}, u32[]{:S(2)}) copy-start(f32[2,32,128]{2,1,0:T(8,128)} %current.3) | copy-start | bytes 98308
  3.8 65.6 %copy-start.9 = (s32[32,6]{0,1:T(8,128)S(1)}, s32[32,6]{0,1:T(8,128)}, u32[]{:S(2)}) copy-start(s32[32,6]{0,1:T(8,128)} %param.14) | copy-start | bytes 2308
  3.8 65.6 %copy-start.12 = (s32[32]{0:T(128)S(1)}, s32[32]{0:T(128)}, u32[]{:S(2)}) copy-start(s32[32]{0:T(128)} %near_count.1) | copy-start | bytes 388
  38.7 44.5 %copy-start.1 = (f32[2,2,32,8,512]{4,3,2,1,0:T(8,128)S(1)}, f32[2,2,32,8,512]{4,3,2,1,0:T(8,128)}, u32[]{:S(2)}) copy-start(f32[2,2,32,8,512]{4,3,2,1,0:T(8,128)} %radiation.3) | copy-start | bytes 6291460
  57.5 25.8 %all-to-all-start.2 = ((f32[16,1,4480]{2,1,0:T(1,128)}), f32[16,1,4480]{2,1,0:T(1,128)S(1)}, u32[]{:S(2)}, u32[]{:S(2)}) async-start(f32[16,1,4480]{2,1,0:T(1,128)} %bitcast.8), calls=%async_computation.2 | async-start | bytes 573440 | tf_op jit(solution)/shard_map/all_to_all | solution.py:245
  64.2 2.9 %collective-permute-start = (f32[2,32,128]{2,1,0:T(8,128)S(1)}, f32[2,32,128]{2,1,0:T(8,128)S(1)}, u32[]{:S(2)}, u32[]{:S(2)}) collective-permute-start(f32[2,32,128]{2,1,0:T(8,128)S(1)} %copy-done.4), channel_id=1, source_target_pairs={{0,16},{16,32},{32,48},{48,64},{64,80},{80,96},{96,112},{112,128},... | collective-permute-start | bytes 98312 | tf_op jit(solution)/shard_map/ppermute | solution.py:195
  65.8 3.6 %collective-permute-start.1 = (f32[2,32,128]{2,1,0:T(8,128)S(1)}, f32[2,32,128]{2,1,0:T(8,128)S(1)}, u32[]{:S(2)}, u32[]{:S(2)}) collective-permute-start(f32[2,32,128]{2,1,0:T(8,128)S(1)} %copy-done.4), channel_id=1, source_target_pairs={{16,0},{32,16},{48,32},{64,48},{80,64},{96,80},{112,96},{128,112},... | collective-permute-start | bytes 98312 | tf_op jit(solution)/shard_map/ppermute | solution.py:196
  69.4 1.4 %copy-start.2 = (f32[2,32,6,8,128]{4,3,2,1,0:T(8,128)S(1)}, f32[2,32,6,8,128]{4,3,2,1,0:T(8,128)}, u32[]{:S(2)}) copy-start(f32[2,32,6,8,128]{4,3,2,1,0:T(8,128)} %blocks.1) | copy-start | bytes 4718596

commit v2 on v1

--- a/solution.py
+++ b/solution.py
@@ -14,30 +14,26 @@
 VMEM = pl.BlockSpec(memory_space=pltpu.VMEM)
 SMEM = pl.BlockSpec(memory_space=pltpu.SMEM)
 ANY = pl.BlockSpec(memory_space=pl.ANY)
+HBM = pl.BlockSpec(memory_space=pltpu.HBM)
 params = pltpu.CompilerParams(vmem_limit_bytes=12 * 2**20)
-
-
-def leaf_kernel(cuts, shares, current, stencil, weight, radiation, out, interp, patterns, columns, rows, samples, sems):
+alone = pltpu.CompilerParams(vmem_limit_bytes=60 * 2**20)
+
+
+def leaf_kernel(cuts, shares, current, radiation, out, patterns, given, columns, rows, samples, sems):
     pols, boxes, own, width = radiation.shape[1:]
-    place = lax.axis_index("dir")
     step = boxes // cuts
+    first = pltpu.make_async_copy(current, given, sems.at[cuts])
+    first.start()
     copies = []
     for cut in range(cuts):
         part = pl.ds(cut * step, step)
         copy = pltpu.make_async_copy(radiation.at[:, :, part], patterns.at[:, :, part], sems.at[cut])
         copy.start()
         copies.append(copy)
-    piece = width // shares
-    lanes = stencil.shape[1]
-    row = lax.broadcasted_iota(jnp.int32, (128, lanes), 0)
-    table = jnp.zeros((128, lanes), f32)
-    for point in range(stencil.shape[0]):
-        at = lax.rem(stencil[point : point + 1, :] - (place * piece - below) + width, width)
-        table = table + jnp.where(row == at, weight[point : point + 1, :], 0.0)
-    interp[...] = table
+    first.wait()
     for part in range(2):
-        columns[part] = current[part].T
-    mine = pl.ds(pl.multiple_of(place * own, own), own)
+        columns[part] = given[part].T
+    mine = pl.ds(pl.multiple_of(lax.axis_index("dir") * own, own), own)
     real, imag = columns[0, mine, :], columns[1, mine, :]
     for cut in range(cuts):
         copies[cut].wait()
@@ -53,13 +49,45 @@
         samples[lead + block * 128 : lead + block * 128 + 128, :] = rows[:, block * 128 : block * 128 + 128].T
     samples[lead - below : lead, :] = samples[lead + width - below : lead + width, :]
     samples[lead + width : lead + width + above, :] = samples[lead : lead + above, :]
+    piece = width // shares
     span = piece + below + above
     for share in range(shares):
-        first = lead - below + share * piece
-        out[share * span : (share + 1) * span, :] = samples[first : first + span, :]
-
-
-def lift_kernel(shares, copies, received, interp, shift, out, total, tops):
+        begin = lead - below + share * piece
+        out[share * span : (share + 1) * span, :] = samples[begin : begin + span, :]
+
+
+def plan_kernel(parents, width, piece, stencil, weight, source, kind, count, translation, interp, picks, factors, codes):
+    lanes = stencil.shape[1]
+    begin = lax.axis_index("dir") * piece - below
+    row = lax.broadcasted_iota(jnp.int32, (128, lanes), 0)
+    table = jnp.zeros((128, lanes), f32)
+    for point in range(stencil.shape[0]):
+        at = lax.rem(stencil[point : point + 1, :] - begin + width, width)
+        table = table + jnp.where(row == at, weight[point : point + 1, :], 0.0)
+    interp[...] = table
+    kinds = translation.shape[1]
+    slots, tops = source.shape
+    lines, columns = picks.shape[0] // (kinds * parents), picks.shape[1]
+    origin = source[...]
+    spot = (origin // parents) * (lines * parents) + lax.rem(origin, parents)
+    live = lax.broadcasted_iota(jnp.int32, (slots, tops), 0) < count[...]
+    codes[...] = jnp.where(live, kind[...] * columns + spot, -1).astype(f32).T
+    mine = codes[pl.ds(lax.axis_index("box") * parents, parents), :]
+    own_kind = lax.broadcasted_iota(jnp.int32, (kinds * parents, slots), 0) // parents
+    mine = jnp.concatenate([mine] * kinds, axis=0) - (own_kind * columns).astype(f32)
+    lane = lax.broadcasted_iota(jnp.int32, (kinds * parents, columns), 1).astype(f32)
+    counts = jnp.zeros((kinds * parents, columns), f32)
+    for slot in range(slots):
+        counts = counts + jnp.where(mine[:, slot : slot + 1] == lane, 1.0, 0.0)
+    parts = [pltpu.roll(counts, line * parents, 1) if line else counts for line in range(lines)]
+    picks[...] = jnp.concatenate(parts, axis=0).astype(jnp.bfloat16)
+    for part in range(2):
+        for which in range(kinds):
+            one = translation[part, which : which + 1, :]
+            factors[part, which * parents : (which + 1) * parents, :] = jnp.broadcast_to(one, (parents, lanes))
+
+
+def lift_kernel(shares, copies, received, interp, shift, near, out, total, tops):
     span = received.shape[0] // shares
     total[...] = jnp.zeros_like(total)
     part = received[0:span, :]
@@ -79,29 +107,31 @@
         out[copy * 2 * lines : (copy + 1) * 2 * lines, :] = value
 
 
-def lower_kernel(shares, span, parents, source, kind, count, received, translation, interp, shift, out, factors, down):
-    kinds = translation.shape[1]
+def lower_kernel(shares, span, parents, picks, factors, received, interp, shift, out, down):
     lines = down.shape[0] // 16
     pols = lines // parents
-    first = lax.axis_index("box") * parents
-    factors[...] = jnp.zeros_like(factors)
-    factors[:, 0:kinds, :] = translation[...]
+    each = factors.shape[1]
+    rest = received[...]
+    table = picks[...]
+    raw = jnp.zeros((table.shape[0], rest.shape[1]), f32)
+    for _ in range(3):
+        part = rest.astype(jnp.bfloat16)
+        raw = raw + jnp.dot(table, part, preferred_element_type=f32)
+        rest = rest - part.astype(f32)
+
+    def over_kinds(line, part):
+        terms = raw[line * each : (line + 1) * each] * factors[part]
+        total = terms[0:parents]
+        for which in range(1, each // parents):
+            total = total + terms[which * parents : (which + 1) * parents]
+        return total
+
     shift_re, shift_im = shift[0], shift[1]
-    for parent in range(parents):
-        used = count[first + parent]
-        by_re = jnp.zeros((2 * pols, 128), f32)
-        by_im = jnp.zeros((2 * pols, 128), f32)
-        for slot in range(source.shape[0]):
-            origin = source[slot, first + parent]
-            which = jnp.where(slot < used, kind[slot, first + parent], kinds)
-            begin = (origin // parents) * (2 * lines) + lax.rem(origin, parents)
-            tops = received[pl.ds(begin, 2 * pols, stride=parents), :]
-            by_re = by_re + tops * factors[0, pl.ds(which, 1), :]
-            by_im = by_im + tops * factors[1, pl.ds(which, 1), :]
-        moved_re = by_re[0:pols] - by_im[pols:]
-        moved_im = by_im[0:pols] + by_re[pols:]
-        for pol in range(pols):
-            mine_re, mine_im = moved_re[pol : pol + 1], moved_im[pol : pol + 1]
+    for pol in range(pols):
+        moved_re = over_kinds(pol, 0) - over_kinds(pols + pol, 1)
+        moved_im = over_kinds(pol, 1) + over_kinds(pols + pol, 0)
+        for parent in range(parents):
+            mine_re, mine_im = moved_re[parent : parent + 1], moved_im[parent : parent + 1]
             at = (pol * parents + parent) * 8
             down[at : at + 8, :] = mine_re * shift_re + mine_im * shift_im
             down[lines * 8 + at : lines * 8 + at + 8, :] = mine_im * shift_re - mine_re * shift_im
@@ -189,39 +219,47 @@
     lanes = 2 * pols * boxes
     held = lead + width + 8
     cuts = 4
-    shape = functools.partial(jax.ShapeDtypeStruct, dtype=f32)
+
+    def shape(dims, dtype=f32):
+        return jax.ShapeDtypeStruct(dims, dtype)
 
     forward = [(i, i + 1) for i in range(box_total - 1)]
     low = lax.ppermute(current, "box", forward)
     high = lax.ppermute(current, "box", [(b, a) for a, b in forward])
 
-    windows, interp = pl.pallas_call(
+    windows = pl.pallas_call(
         functools.partial(leaf_kernel, cuts, dir_total),
-        out_shape=(shape((dir_total * span, lanes)), shape((128, share))),
-        in_specs=[VMEM, VMEM, VMEM, ANY],
-        out_specs=(VMEM, VMEM),
+        out_shape=shape((dir_total * span, lanes)),
+        in_specs=[HBM, HBM],
+        out_specs=VMEM,
         scratch_shapes=[
             pltpu.VMEM(radiation.shape, f32),
+            pltpu.VMEM(current.shape, f32),
             pltpu.VMEM((2, current.shape[2], boxes), f32),
             pltpu.VMEM((lanes, width), f32),
             pltpu.VMEM((held, lanes), f32),
-            pltpu.SemaphoreType.DMA((cuts,)),
+            pltpu.SemaphoreType.DMA((cuts + 1,)),
         ],
-        compiler_params=params,
+        compiler_params=alone,
         name="leaf",
-    )(current, stencil.T, stencil_weight.T, radiation)
+    )(current, radiation)
     windows = lax.all_to_all(windows.reshape(dir_total, 1, span * lanes), "dir", 0, 0, tiled=True)
 
-    tops = pl.pallas_call(
-        functools.partial(lift_kernel, dir_total, box_total),
-        out_shape=shape((box_total * lanes // 8, share)),
-        in_specs=[VMEM] * 3,
-        out_specs=VMEM,
-        scratch_shapes=[pltpu.VMEM((128, lanes), f32), pltpu.VMEM((lanes // 8, share), f32)],
-        compiler_params=params,
-        name="lift",
-    )(windows.reshape(dir_total * span, lanes), interp, child_shift)
-    tops = lax.all_to_all(tops.reshape(box_total, 1, lanes // 8 * share), "box", 0, 0, tiled=True)
+    kinds, tops_total = translation.shape[1], list_source.shape[0]
+    interp, picks, factors = pl.pallas_call(
+        functools.partial(plan_kernel, parents, width, piece),
+        out_shape=(
+            shape((128, share)),
+            shape((2 * pols * kinds * parents, box_total * lanes // 8), dtype=jnp.bfloat16),
+            shape((2, kinds * parents, share)),
+        ),
+        in_specs=[VMEM] * 6,
+        out_specs=(VMEM, VMEM, VMEM),
+        scratch_shapes=[pltpu.VMEM((tops_total, list_source.shape[1]), f32)],
+        compiler_params=params,
+        cost_estimate=pl.CostEstimate(flops=2_000_000, bytes_accessed=2_000_000, transcendentals=0),
+        name="plan",
+    )(stencil.T, stencil_weight.T, list_source.T, list_kind.T, list_count.reshape(1, -1), translation)
 
     near = pl.pallas_call(
         near_kernel,
@@ -230,18 +268,30 @@
         out_specs=VMEM,
         scratch_shapes=[pltpu.VMEM((2, 3 * boxes + 8, 128), f32)],
         compiler_params=params,
+        cost_estimate=pl.CostEstimate(flops=4_000_000, bytes_accessed=4_000_000, transcendentals=0),
         name="near",
     )(neighbours.T, near_count, low, current, high, near_block)
+
+    tops = pl.pallas_call(
+        functools.partial(lift_kernel, dir_total, box_total),
+        out_shape=shape((box_total * lanes // 8, share)),
+        in_specs=[VMEM] * 3 + [ANY],
+        out_specs=VMEM,
+        scratch_shapes=[pltpu.VMEM((128, lanes), f32), pltpu.VMEM((lanes // 8, share), f32)],
+        compiler_params=params,
+        name="lift",
+    )(windows.reshape(dir_total * span, lanes), interp, child_shift, near)
+    tops = lax.all_to_all(tops.reshape(box_total, 1, lanes // 8 * share), "box", 0, 0, tiled=True)
 
     income = pl.pallas_call(
         functools.partial(lower_kernel, dir_total, span, parents),
         out_shape=shape((dir_total * span, lanes)),
-        in_specs=[SMEM] * 3 + [VMEM] * 4,
-        out_specs=VMEM,
-        scratch_shapes=[pltpu.VMEM((2, 16, share), f32), pltpu.VMEM((lanes, share), f32)],
+        in_specs=[VMEM] * 5,
+        out_specs=VMEM,
+        scratch_shapes=[pltpu.VMEM((lanes, share), f32)],
         compiler_params=params,
         name="lower",
-    )(list_source.T, list_kind.T, list_count, tops.reshape(-1, share), translation, interp, child_shift)
+    )(picks, factors, tops.reshape(-1, share), interp, child_shift)
     income = lax.all_to_all(income.reshape(dir_total, 1, span * lanes), "dir", 0, 0, tiled=True)
 
     field = pl.pallas_call(

time: 84.8 us -> 81 us (0.955)
  starting transfers between devices: 9.63 us -> 17.8 us
  blocking collectives: 49.7 us -> 41.7 us
  local copies, waits for them, and re-layouts: 5.17 us -> 1.45 us
    all_to_all x1, starting transfers between devices: 6.72 us -> 15.2 us  [local(): lax.all_to_all(windows.reshape(dir_total, 1, span * lanes), 'dir', 0, 0,...]
    all_to_all x1, blocking collectives: 33.5 us -> 25.7 us  [local(): lax.all_to_all(income.reshape(dir_total, 1, span * lanes), 'dir', 0, 0, t...]
    unnamed x28 -> x24, local copies, waits for them, and re-layouts: 5.17 us -> 1.45 us
    pallas_call x1, Pallas kernels: 2.23 us -> 0.62 us  [local(): pl.pallas_call(functools.partial(lower_kernel, dir_total, span, parents),...]
    pallas_call x1, Pallas kernels: 1.46 us -> 3.05 us  [local(): pl.pallas_call(functools.partial(leaf_kernel, cuts, dir_total), out_shape...]
    all_to_all x1, waiting for transfers between devices: 11.5 us -> 9.98 us  [local(): lax.all_to_all(windows.reshape(dir_total, 1, span * lanes), 'dir', 0, 0,...]
  transfers between devices with their start and end apart: 3 -> 3, of which waited for: 2 -> 2; matrix products, arithmetic and copies ran while one was open for 0% -> 0% of each run, Pallas kernels for 1% -> 2%
where the time goes in v2:
time: 81 us; the launch traced here: 80.7 us
  blocking collectives  41.7 us (51%)
  starting transfers between devices  17.8 us (22%)
  waiting for transfers between devices  13 us (16%)
  Pallas kernels  6.53 us (8%)
  local copies, waits for them, and re-layouts  1.45 us (2%)
    all_to_all x1, blocking collectives, local(): lax.all_to_all(income.reshape(dir_total, 1, span * lanes), 'dir', 0, 0, t...  25.7 us
    all_to_all x1, blocking collectives, local(): lax.all_to_all(tops.reshape(box_total, 1, lanes // 8 * share), 'box', 0,...  16 us
    all_to_all x1, starting transfers between devices, local(): lax.all_to_all(windows.reshape(dir_total, 1, span * lanes), 'dir', 0, 0,...  15.2 us
    all_to_all x1, waiting for transfers between devices, local(): lax.all_to_all(windows.reshape(dir_total, 1, span * lanes), 'dir', 0, 0,...  9.98 us
    ppermute x1, waiting for transfers between devices, local(): high = lax.ppermute(current, 'box', [(b, a) for a, b in forward])  3.06 us
    pallas_call x1, Pallas kernels, local(): pl.pallas_call(functools.partial(leaf_kernel, cuts, dir_total), out_shape...  3.05 us
  transfers between devices with their start and end apart: 3, of which 2 were waited for; matrix products, arithmetic and copies ran while one was open for 0% of the time, Pallas kernels for 2%

profile of v2, /device:TPU:32, one launch (start us, length us, event | category | flops | bytes accessed | tf_op | source)
XLA Modules:
  0.0 80.7 jit_solution(6436419780500639655)
XLA Ops:
  0.0 0.0 copy-start.4
  0.0 0.0 copy-start.5
  0.0 0.0 copy-start.10
  0.0 0.0 copy-start.6
  0.0 0.0 copy-start.7
  0.1 0.0 copy-start.11
  0.1 0.0 copy-start.3
  0.1 3.1 %leaf.1 = f32[560,128]{1,0:T(8,128)} custom-call(f32[2,32,128]{2,1,0:T(8,128)} %current.3, f32[2,2,32,8,512]{4,3,2,1,0:T(8,128)} %radiation.3), custom_call_target="tpu_custom_call" | custom-call | tf_op jit(solution)/shard_map/leaf/pallas_call | solution.py:230
  3.1 15.2 %all-to-all-start = ((f32[16,1,4480]{2,1,0:T(1,128)}), f32[16,1,4480]{2,1,0:T(1,128)S(1)}, u32[]{:S(2)}, u32[]{:S(2)}) async-start(f32[16,1,4480]{2,1,0:T(1,128)} %bitcast.24), calls=%async_computation | async-start | bytes 573440 | tf_op jit(solution)/shard_map/all_to_all | solution.py:246
  18.4 0.0 copy-done.2
  18.4 1.3 %collective-permute-start = (f32[2,32,128]{2,1,0:T(8,128)S(1)}, f32[2,32,128]{2,1,0:T(8,128)S(1)}, u32[]{:S(2)}, u32[]{:S(2)}) collective-permute-start(f32[2,32,128]{2,1,0:T(8,128)S(1)} %copy-done.2), channel_id=1, source_target_pairs={{0,16},{16,32},{32,48},{48,64},{64,80},{80,96},{96,112},{112,128},... | collective-permute-start | bytes 98312 | tf_op jit(solution)/shard_map/ppermute | solution.py:227
  19.7 1.3 %collective-permute-start.1 = (f32[2,32,128]{2,1,0:T(8,128)S(1)}, f32[2,32,128]{2,1,0:T(8,128)S(1)}, u32[]{:S(2)}, u32[]{:S(2)}) collective-permute-start(f32[2,32,128]{2,1,0:T(8,128)S(1)} %copy-done.2), channel_id=1, source_target_pairs={{16,0},{32,16},{48,32},{64,48},{80,64},{96,80},{112,96},{128,112},... | collective-permute-start | bytes 98312 | tf_op jit(solution)/shard_map/ppermute | solution.py:228
  21.0 0.0 copy-done.8
  21.0 0.4 plan.1
  21.4 0.0 collective-permute-done.low
  21.4 3.1 %collective-permute-done.1.high = f32[2,32,128]{2,1,0:T(8,128)S(1)} collective-permute-done((f32[2,32,128]{2,1,0:T(8,128)S(1)}, f32[2,32,128]{2,1,0:T(8,128)S(1)}, u32[]{:S(2)}, u32[]{:S(2)}) %collective-permute-start.1) | collective-permute-done | bytes 32800 | tf_op jit(solution)/shard_map/ppermute | solution.py:228
  24.5 1.4 %copy-done.1 = f32[2,32,6,8,128]{4,3,2,1,0:T(8,128)S(1)} copy-done((f32[2,32,6,8,128]{4,3,2,1,0:T(8,128)S(1)}, f32[2,32,6,8,128]{4,3,2,1,0:T(8,128)}, u32[]{:S(2)}) %copy-start.1) | copy-done | bytes 1572888
  25.9 0.9 %near.1 = f32[2,32,8,128]{3,2,1,0:T(8,128)S(1)} custom-call(s32[6,32]{1,0:T(8,128)S(1)} %bitcast.20, s32[32]{0:T(128)S(1)} %copy-done.11, f32[2,32,128]{2,1,0:T(8,128)S(1)} %collective-permute-done.low, f32[2,32,128]{2,1,0:T(8,128)S(1)} %copy-done.2, f32[2,32,128]{2,1,0:T(8,128)S(1)} %collective-permute-done.1.high, f32[2,32,6,8,128]{4,3,2,1,0:T(8,128)S(1)} %copy-done.1), custom_call_target="tpu_custom_call" | custom-call | flops 4000000 | bytes 4000000 | tf_op jit(solution)/shard_map/near/pallas_call | solution.py:264
  26.8 10.0 %all-to-all-done = f32[16,1,4480]{2,1,0:T(1,128)S(1)} async-done(((f32[16,1,4480]{2,1,0:T(1,128)}), f32[16,1,4480]{2,1,0:T(1,128)S(1)}, u32[]{:S(2)}, u32[]{:S(2)}) %all-to-all-start) | async-done | bytes 286752 | tf_op jit(solution)/shard_map/all_to_all | solution.py:246
  36.8 0.3 lift.1
  37.1 16.0 %all_to_all.15 = f32[32,1,2048]{2,1,0:T(1,128)S(1)} all-to-all(f32[32,1,2048]{2,1,0:T(1,128)S(1)} %bitcast.17), channel_id=1, replica_groups=mesh['box'=32,'dir'=16] {'box'}, dimensions={0} | all-to-all | bytes 524288 | tf_op jit(solution)/shard_map/all_to_all | solution.py:284
  53.1 0.6 lower.1
  53.8 25.7 %all_to_all.16 = f32[16,1,4480]{2,1,0:T(1,128)S(1)} all-to-all(f32[16,1,4480]{2,1,0:T(1,128)S(1)} %bitcast.14), channel_id=1, replica_groups=mesh['box'=32,'dir'=16] {'dir'}, dimensions={0} | all-to-all | bytes 573440 | tf_op jit(solution)/shard_map/all_to_all | solution.py:295
  79.4 1.3 %field.1 = f32[2,8,32]{2,1,0:T(8,128)} custom-call(f32[560,128]{1,0:T(8,128)S(1)} %bitcast.15, f32[2,2,32,8,512]{4,3,2,1,0:T(8,128)S(1)} %copy-done, f32[2,32,8,128]{3,2,1,0:T(8,128)S(1)} %near.1), custom_call_target="tpu_custom_call" | custom-call | tf_op jit(solution)/shard_map/field/pallas_call | solution.py:297
  (14 shorter events, 0.0 us)
Async XLA Ops:
  0.0 18.4 %copy-start.2 = (f32[2,32,128]{2,1,0:T(8,128)S(1)}, f32[2,32,128]{2,1,0:T(8,128)}, u32[]{:S(2)}) copy-start(f32[2,32,128]{2,1,0:T(8,128)} %current.3) | copy-start | bytes 98308
  0.0 21.0 %copy-start.8 = (s32[128,4]{0,1:T(4,128)S(1)}, s32[128,4]{0,1:T(4,128)}, u32[]{:S(2)}) copy-start(s32[128,4]{0,1:T(4,128)} %param.17) | copy-start | bytes 6148
  0.0 21.0 %copy-start.9 = (f32[128,4]{0,1:T(4,128)S(1)}, f32[128,4]{0,1:T(4,128)}, u32[]{:S(2)}) copy-start(f32[128,4]{0,1:T(4,128)} %param.18) | copy-start | bytes 6148
  0.0 21.0 %copy-start.4 = (s32[128,16]{0,1:T(8,128)S(1)}, s32[128,16]{0,1:T(8,128)}, u32[]{:S(2)}) copy-start(s32[128,16]{0,1:T(8,128)} %param.20) | copy-start | bytes 24580
  0.0 21.0 %copy-start.5 = (s32[128,16]{0,1:T(8,128)S(1)}, s32[128,16]{0,1:T(8,128)}, u32[]{:S(2)}) copy-start(s32[128,16]{0,1:T(8,128)} %param.21) | copy-start | bytes 24580
  0.0 21.0 %copy-start.10 = (s32[128]{0:T(128)S(1)}, s32[128]{0:T(128)}, u32[]{:S(2)}) copy-start(s32[128]{0:T(128)} %param.22) | copy-start | bytes 1540
  0.0 21.0 %copy-start.6 = (f32[2,8,128]{2,1,0:T(8,128)S(1)}, f32[2,8,128]{2,1,0:T(8,128)}, u32[]{:S(2)}) copy-start(f32[2,8,128]{2,1,0:T(8,128)} %translation.1) | copy-start | bytes 24580
  0.0 24.4 %copy-start.7 = (s32[32,6]{0,1:T(8,128)S(1)}, s32[32,6]{0,1:T(8,128)}, u32[]{:S(2)}) copy-start(s32[32,6]{0,1:T(8,128)} %param.14) | copy-start | bytes 2308
  0.1 24.4 %copy-start.11 = (s32[32]{0:T(128)S(1)}, s32[32]{0:T(128)}, u32[]{:S(2)}) copy-start(s32[32]{0:T(128)} %near_count.1) | copy-start | bytes 388
  0.1 36.7 %copy-start.3 = (f32[2,8,128]{2,1,0:T(8,128)S(1)}, f32[2,8,128]{2,1,0:T(8,128)}, u32[]{:S(2)}) copy-start(f32[2,8,128]{2,1,0:T(8,128)} %shift.3) | copy-start | bytes 24580
  3.1 33.6 %all-to-all-start = ((f32[16,1,4480]{2,1,0:T(1,128)}), f32[16,1,4480]{2,1,0:T(1,128)S(1)}, u32[]{:S(2)}, u32[]{:S(2)}) async-start(f32[16,1,4480]{2,1,0:T(1,128)} %bitcast.24), calls=%async_computation | async-start | bytes 573440 | tf_op jit(solution)/shard_map/all_to_all | solution.py:246
  18.4 3.1 %collective-permute-start = (f32[2,32,128]{2,1,0:T(8,128)S(1)}, f32[2,32,128]{2,1,0:T(8,128)S(1)}, u32[]{:S(2)}, u32[]{:S(2)}) collective-permute-start(f32[2,32,128]{2,1,0:T(8,128)S(1)} %copy-done.2), channel_id=1, source_target_pairs={{0,16},{16,32},{32,48},{48,64},{64,80},{80,96},{96,112},{112,128},... | collective-permute-start | bytes 98312 | tf_op jit(solution)/shard_map/ppermute | solution.py:227
  19.7 4.8 %collective-permute-start.1 = (f32[2,32,128]{2,1,0:T(8,128)S(1)}, f32[2,32,128]{2,1,0:T(8,128)S(1)}, u32[]{:S(2)}, u32[]{:S(2)}) collective-permute-start(f32[2,32,128]{2,1,0:T(8,128)S(1)} %copy-done.2), channel_id=1, source_target_pairs={{16,0},{32,16},{48,32},{64,48},{80,64},{96,80},{112,96},{128,112},... | collective-permute-start | bytes 98312 | tf_op jit(solution)/shard_map/ppermute | solution.py:228
  24.5 1.4 %copy-start.1 = (f32[2,32,6,8,128]{4,3,2,1,0:T(8,128)S(1)}, f32[2,32,6,8,128]{4,3,2,1,0:T(8,128)}, u32[]{:S(2)}) copy-start(f32[2,32,6,8,128]{4,3,2,1,0:T(8,128)} %blocks.1) | copy-start | bytes 4718596
  25.9 53.5 %copy-start = (f32[2,2,32,8,512]{4,3,2,1,0:T(8,128)S(1)}, f32[2,2,32,8,512]{4,3,2,1,0:T(8,128)}, u32[]{:S(2)}) copy-start(f32[2,2,32,8,512]{4,3,2,1,0:T(8,128)} %radiation.3) | copy-start | bytes 6291460

commit v3 on v2

--- a/solution.py
+++ b/solution.py
@@ -11,6 +11,7 @@
 f32 = jnp.float32
 below, above = 1, 2
 lead = 8
+reach = below + above + 1
 VMEM = pl.BlockSpec(memory_space=pltpu.VMEM)
 SMEM = pl.BlockSpec(memory_space=pltpu.SMEM)
 ANY = pl.BlockSpec(memory_space=pl.ANY)
@@ -19,21 +20,41 @@
 alone = pltpu.CompilerParams(vmem_limit_bytes=60 * 2**20)
 
 
-def leaf_kernel(cuts, shares, current, radiation, out, patterns, given, columns, rows, samples, sems):
+def leaf_kernel(cuts, shares, total, spare, current, stencil, weight, shift, radiation, out, patterns, *scratch):
+    given, points, weights, shifts, tables, columns, rows, samples, sems = scratch
     pols, boxes, own, width = radiation.shape[1:]
     step = boxes // cuts
-    first = pltpu.make_async_copy(current, given, sems.at[cuts])
-    first.start()
+    small = [
+        pltpu.make_async_copy(source, target, sems.at[cuts + index])
+        for index, (source, target) in enumerate(((current, given), (stencil, points), (weight, weights), (shift, shifts)))
+    ]
+    for copy in small:
+        copy.start()
     copies = []
     for cut in range(cuts):
         part = pl.ds(cut * step, step)
         copy = pltpu.make_async_copy(radiation.at[:, :, part], patterns.at[:, :, part], sems.at[cut])
         copy.start()
         copies.append(copy)
-    first.wait()
+    for copy in small:
+        copy.wait()
     for part in range(2):
         columns[part] = given[part].T
-    mine = pl.ds(pl.multiple_of(lax.axis_index("dir") * own, own), own)
+    place = lax.axis_index("dir")
+    mine = pl.ds(pl.multiple_of(place * own, own), own)
+    piece = width // shares
+    lanes = stencil.shape[1]
+    tables[0:8, :] = shifts[0]
+    tables[8:16, :] = shifts[1]
+    tables[16:, :] = jnp.zeros((tables.shape[0] - 16, lanes), f32)
+    centre = place * piece - below + lax.broadcasted_iota(jnp.int32, (1, lanes), 1) // (lanes // piece)
+    for offset in range(reach):
+        line = jnp.zeros((1, lanes), f32)
+        for point in range(stencil.shape[0]):
+            at = lax.rem(points[point : point + 1, :] - centre + width, width)
+            line = line + jnp.where(at == offset, weights[point : point + 1, :], 0.0)
+        tables[16 + offset : 17 + offset, :] = line
+    begin = lax.rem(lax.axis_index("box") + total - lax.rem(place * (16 + reach), total), total)
     real, imag = columns[0, mine, :], columns[1, mine, :]
     for cut in range(cuts):
         copies[cut].wait()
@@ -49,11 +70,13 @@
         samples[lead + block * 128 : lead + block * 128 + 128, :] = rows[:, block * 128 : block * 128 + 128].T
     samples[lead - below : lead, :] = samples[lead + width - below : lead + width, :]
     samples[lead + width : lead + width + above, :] = samples[lead : lead + above, :]
-    piece = width // shares
     span = piece + below + above
+    own_rows = [tables[pl.ds(begin + index * total, 1), :] for index in range(spare)]
     for share in range(shares):
-        begin = lead - below + share * piece
-        out[share * span : (share + 1) * span, :] = samples[begin : begin + span, :]
+        first, at = lead - below + share * piece, share * (span + spare)
+        out[at : at + span, :] = samples[first : first + span, :]
+        for index in range(spare):
+            out[at + span + index : at + span + index + 1, :] = own_rows[index]
 
 
 def plan_kernel(parents, width, piece, stencil, weight, source, kind, count, translation, interp, picks, factors, codes):
@@ -87,12 +110,13 @@
             factors[part, which * parents : (which + 1) * parents, :] = jnp.broadcast_to(one, (parents, lanes))
 
 
-def lift_kernel(shares, copies, received, interp, shift, near, out, total, tops):
-    span = received.shape[0] // shares
+def lift_kernel(shares, copies, spare, received, interp, shift, near, out, total, tops):
+    each = received.shape[0] // shares
+    span = each - spare
     total[...] = jnp.zeros_like(total)
     part = received[0:span, :]
     for share in range(1, shares):
-        part = part + received[share * span : (share + 1) * span, :]
+        part = part + received[share * each : share * each + span, :]
     total[0:span, :] = part
     up = jnp.dot(total[...].T, interp[...], precision=highest, preferred_element_type=f32)
     shift_re, shift_im = shift[0], shift[1]
@@ -102,16 +126,28 @@
         up_re, up_im = up[line * 8 : line * 8 + 8], up[half + line * 8 : half + line * 8 + 8]
         tops[line : line + 1, :] = jnp.sum(up_re * shift_re - up_im * shift_im, axis=0, keepdims=True)
         tops[lines + line : lines + line + 1, :] = jnp.sum(up_re * shift_im + up_im * shift_re, axis=0, keepdims=True)
+    height = tops.shape[0]
+    place = lax.axis_index("box")
+    for index in range(height - 2 * lines):
+        number = place + index * copies
+        share = number // (16 + reach)
+        at = share * each + span + (number - share * (16 + reach)) // copies
+        tops[2 * lines + index : 2 * lines + index + 1, :] = received[pl.ds(at, 1), :]
     value = tops[...]
     for copy in range(copies):
-        out[copy * 2 * lines : (copy + 1) * 2 * lines, :] = value
-
-
-def lower_kernel(shares, span, parents, picks, factors, received, interp, shift, out, down):
-    lines = down.shape[0] // 16
-    pols = lines // parents
+        out[copy * height : (copy + 1) * height, :] = value
+
+
+def lower_kernel(shares, parents, picks, factors, gathered, out, compact):
     each = factors.shape[1]
-    rest = received[...]
+    lines = picks.shape[0] // each
+    pols = lines // 2
+    height = lines * parents
+    boxes = compact.shape[0] // height
+    stride = gathered.shape[0] // boxes
+    for box in range(boxes):
+        compact[box * height : (box + 1) * height, :] = gathered[box * stride : box * stride + height, :]
+    rest = compact[...]
     table = picks[...]
     raw = jnp.zeros((table.shape[0], rest.shape[1]), f32)
     for _ in range(3):
@@ -126,21 +162,11 @@
             total = total + terms[which * parents : (which + 1) * parents]
         return total
 
-    shift_re, shift_im = shift[0], shift[1]
-    for pol in range(pols):
-        moved_re = over_kinds(pol, 0) - over_kinds(pols + pol, 1)
-        moved_im = over_kinds(pol, 1) + over_kinds(pols + pol, 0)
-        for parent in range(parents):
-            mine_re, mine_im = moved_re[parent : parent + 1], moved_im[parent : parent + 1]
-            at = (pol * parents + parent) * 8
-            down[at : at + 8, :] = mine_re * shift_re + mine_im * shift_im
-            down[lines * 8 + at : lines * 8 + at + 8, :] = mine_im * shift_re - mine_re * shift_im
-    settled = lax.dot_general(
-        interp[0:40, :], down[...], (((1,), (1,)), ((), ())), precision=highest, preferred_element_type=f32
-    )
-    value = settled[0:span]
+    moved = [over_kinds(pol, 0) - over_kinds(pols + pol, 1) for pol in range(pols)]
+    moved += [over_kinds(pol, 1) + over_kinds(pols + pol, 0) for pol in range(pols)]
+    value = jnp.concatenate(moved, axis=0)
     for share in range(shares):
-        out[share * span : (share + 1) * span, :] = value
+        out[share * height : (share + 1) * height, :] = value
 
 
 def near_kernel(neighbours, near_count, low, current, high, blocks, out, padded):
@@ -165,14 +191,60 @@
         out[1, box] = sum_im
 
 
-def field_kernel(shares, received, radiation, near, out, samples, rows):
+def field_kernel(shares, total, received, gathered, radiation, near, out, samples, rows, down):
     pols, boxes, own, width = radiation.shape[1:]
-    span = received.shape[0] // shares
     piece = width // shares
+    height = received.shape[0] // shares
+    half, tall = height // 2, down.shape[0] // 2
+    stride = gathered.shape[0] // total
+    lanes = received.shape[1]
+
+    def table_row(number):
+        return number % total * stride + height + number // total
+
+    def octants(number):
+        ends = [number]
+        for one in range(number + 1, number + 8):
+            if one % total == 0:
+                ends.append(one)
+        ends.append(number + 8)
+        parts = []
+        for low, high in zip(ends[:-1], ends[1:]):
+            if high - low == 1:
+                parts.append(gathered[table_row(low) : table_row(low) + 1, :])
+            else:
+                parts.append(gathered[pl.ds(table_row(low), high - low, stride=stride), :])
+        return parts[0] if len(parts) == 1 else jnp.concatenate(parts, axis=0)
+
     samples[...] = jnp.zeros_like(samples)
+    sample = lax.broadcasted_iota(jnp.int32, (40, lanes), 0)
+    offset = sample - lax.broadcasted_iota(jnp.int32, (40, lanes), 1) // (lanes // piece)
+    contract = (((1,), (1,)), ((), ()))
     for share in range(shares):
+        number = share * (16 + reach)
+        shift_re, shift_im = octants(number), octants(number + 8)
+        table = jnp.zeros((40, lanes), f32)
+        for step in range(reach):
+            at = table_row(number + 16 + step)
+            table = jnp.where(offset == step, gathered[at : at + 1, :], table)
+        for line in range(half):
+            at = share * height + line
+            moved_re, moved_im = received[at : at + 1, :], received[at + half : at + half + 1, :]
+            down[line * 8 : line * 8 + 8, :] = moved_re * shift_re + moved_im * shift_im
+            down[tall + line * 8 : tall + line * 8 + 8, :] = moved_im * shift_re - moved_re * shift_im
+        value = down[...]
+        value_hi = value.astype(jnp.bfloat16)
+        value_lo = (value - value_hi.astype(f32)).astype(jnp.bfloat16)
+        table_hi = table.astype(jnp.bfloat16)
+        table_lo = (table - table_hi.astype(f32)).astype(jnp.bfloat16)
+        settled = lax.dot_general(
+            jnp.concatenate([table_hi, table_hi], axis=1),
+            jnp.concatenate([value_hi, value_lo], axis=1),
+            contract,
+            preferred_element_type=f32,
+        ) + lax.dot_general(table_lo, value_hi, contract, preferred_element_type=f32)
         first = lead - below + share * piece
-        samples[first : first + span, :] += received[share * span : (share + 1) * span, :]
+        samples[first : first + 40, :] += settled
     samples[lead + width - below : lead + width, :] += samples[lead - below : lead, :]
     samples[lead : lead + above, :] += samples[lead + width : lead + width + above, :]
     for block in range(width // 128):
@@ -219,6 +291,8 @@
     lanes = 2 * pols * boxes
     held = lead + width + 8
     cuts = 4
+    spare = -(-(16 + reach) // box_total)
+    height = lanes // 8 + (16 + reach) * dir_total // box_total
 
     def shape(dims, dtype=f32):
         return jax.ShapeDtypeStruct(dims, dtype)
@@ -228,22 +302,26 @@
     high = lax.ppermute(current, "box", [(b, a) for a, b in forward])
 
     windows = pl.pallas_call(
-        functools.partial(leaf_kernel, cuts, dir_total),
-        out_shape=shape((dir_total * span, lanes)),
-        in_specs=[HBM, HBM],
+        functools.partial(leaf_kernel, cuts, dir_total, box_total, spare),
+        out_shape=shape((dir_total * (span + spare), lanes)),
+        in_specs=[HBM] * 5,
         out_specs=VMEM,
         scratch_shapes=[
             pltpu.VMEM(radiation.shape, f32),
             pltpu.VMEM(current.shape, f32),
+            pltpu.VMEM((stencil.shape[1], share), jnp.int32),
+            pltpu.VMEM((stencil.shape[1], share), f32),
+            pltpu.VMEM(child_shift.shape, f32),
+            pltpu.VMEM((spare * box_total + 16 + reach, share), f32),
             pltpu.VMEM((2, current.shape[2], boxes), f32),
             pltpu.VMEM((lanes, width), f32),
             pltpu.VMEM((held, lanes), f32),
-            pltpu.SemaphoreType.DMA((cuts + 1,)),
+            pltpu.SemaphoreType.DMA((cuts + 4,)),
         ],
         compiler_params=alone,
         name="leaf",
-    )(current, radiation)
-    windows = lax.all_to_all(windows.reshape(dir_total, 1, span * lanes), "dir", 0, 0, tiled=True)
+    )(current, stencil.T, stencil_weight.T, child_shift, radiation)
+    windows = lax.all_to_all(windows.reshape(dir_total, 1, (span + spare) * lanes), "dir", 0, 0, tiled=True)
 
     kinds, tops_total = translation.shape[1], list_source.shape[0]
     interp, picks, factors = pl.pallas_call(
@@ -273,36 +351,37 @@
     )(neighbours.T, near_count, low, current, high, near_block)
 
     tops = pl.pallas_call(
-        functools.partial(lift_kernel, dir_total, box_total),
-        out_shape=shape((box_total * lanes // 8, share)),
+        functools.partial(lift_kernel, dir_total, box_total, spare),
+        out_shape=shape((box_total * height, share)),
         in_specs=[VMEM] * 3 + [ANY],
         out_specs=VMEM,
-        scratch_shapes=[pltpu.VMEM((128, lanes), f32), pltpu.VMEM((lanes // 8, share), f32)],
+        scratch_shapes=[pltpu.VMEM((128, lanes), f32), pltpu.VMEM((height, share), f32)],
         compiler_params=params,
         name="lift",
-    )(windows.reshape(dir_total * span, lanes), interp, child_shift, near)
-    tops = lax.all_to_all(tops.reshape(box_total, 1, lanes // 8 * share), "box", 0, 0, tiled=True)
-
-    income = pl.pallas_call(
-        functools.partial(lower_kernel, dir_total, span, parents),
-        out_shape=shape((dir_total * span, lanes)),
-        in_specs=[VMEM] * 5,
+    )(windows.reshape(dir_total * (span + spare), lanes), interp, child_shift, near)
+    gathered = lax.all_to_all(tops.reshape(box_total, 1, height * share), "box", 0, 0, tiled=True)
+    gathered = gathered.reshape(box_total * height, share)
+
+    moved = pl.pallas_call(
+        functools.partial(lower_kernel, dir_total, parents),
+        out_shape=shape((dir_total * lanes // 8, share)),
+        in_specs=[VMEM] * 3,
         out_specs=VMEM,
-        scratch_shapes=[pltpu.VMEM((lanes, share), f32)],
+        scratch_shapes=[pltpu.VMEM((box_total * lanes // 8, share), f32)],
         compiler_params=params,
         name="lower",
-    )(picks, factors, tops.reshape(-1, share), interp, child_shift)
-    income = lax.all_to_all(income.reshape(dir_total, 1, span * lanes), "dir", 0, 0, tiled=True)
+    )(picks, factors, gathered)
+    moved = lax.all_to_all(moved.reshape(dir_total, 1, lanes // 8 * share), "dir", 0, 0, tiled=True)
 
     field = pl.pallas_call(
-        functools.partial(field_kernel, dir_total),
+        functools.partial(field_kernel, dir_total, box_total),
         out_shape=shape((2, own, boxes)),
-        in_specs=[VMEM] * 3,
+        in_specs=[VMEM] * 4,
         out_specs=VMEM,
-        scratch_shapes=[pltpu.VMEM((held, lanes), f32), pltpu.VMEM((lanes, width), f32)],
+        scratch_shapes=[pltpu.VMEM((held, lanes), f32), pltpu.VMEM((lanes, width), f32), pltpu.VMEM((lanes, share), f32)],
         compiler_params=params,
         name="field",
-    )(income.reshape(dir_total * span, lanes), radiation, near)
+    )(moved.reshape(dir_total * lanes // 8, share), gathered, radiation, near)
     return field.transpose(0, 2, 1)
 
 

time: 81 us -> 78.4 us (0.968)
  blocking collectives: 41.7 us -> 38.3 us
    all_to_all x2, blocking collectives: 41.7 us -> 38.3 us  [the longest x1 20.5 us: local(): lax.all_to_all(moved.reshape(dir_total, 1, lanes // 8 * share), 'dir', 0,...]
where the time goes in v3:
time: 78.4 us; the launch traced here: 78.1 us
  blocking collectives  38.3 us (49%)
  starting transfers between devices  17.8 us (23%)
  waiting for transfers between devices  13.4 us (17%)
  Pallas kernels  6.94 us (9%)
  local copies, waits for them, and re-layouts  1.45 us (2%)
    all_to_all x1, blocking collectives, local(): lax.all_to_all(moved.reshape(dir_total, 1, lanes // 8 * share), 'dir', 0,...  20.5 us
    all_to_all x1, blocking collectives, local(): lax.all_to_all(tops.reshape(box_total, 1, height * share), 'box', 0, 0, t...  17.8 us
    all_to_all x1, starting transfers between devices, local(): lax.all_to_all(windows.reshape(dir_total, 1, (span + spare) * lanes), 'di...  15.2 us
    all_to_all x1, waiting for transfers between devices, local(): lax.all_to_all(windows.reshape(dir_total, 1, (span + spare) * lanes), 'di...  10.3 us
    pallas_call x1, Pallas kernels, local(): pl.pallas_call(functools.partial(leaf_kernel, cuts, dir_total, box_total,...  3.12 us
    ppermute x1, waiting for transfers between devices, local(): high = lax.ppermute(current, 'box', [(b, a) for a, b in forward])  3.06 us
    pallas_call x1, Pallas kernels, local(): pl.pallas_call(functools.partial(field_kernel, dir_total, box_total), out...  1.94 us
  transfers between devices with their start and end apart: 3, of which 2 were waited for; matrix products, arithmetic and copies ran while one was open for 0% of the time, Pallas kernels for 2%

profile of v3, /device:TPU:32, one launch (start us, length us, event | category | flops | bytes accessed | tf_op | source)
XLA Modules:
  0.0 78.1 jit_solution(8008193797281847025)
XLA Ops:
  0.1 3.1 %leaf.1 = f32[576,128]{1,0:T(8,128)} custom-call(f32[2,32,128]{2,1,0:T(8,128)} %current.3, s32[4,128]{1,0:T(4,128)} %bitcast.19, f32[4,128]{1,0:T(4,128)} %bitcast.21, f32[2,8,128]{2,1,0:T(8,128)} %shift.3, f32[2,2,32,8,512]{4,3,2,1,0:T(8,128)} %radiation.3), custom_call_target="tpu_custom_call" | custom-call | tf_op jit(solution)/shard_map/leaf/pallas_call | solution.py:304
  3.2 15.2 %all-to-all-start = ((f32[16,1,4608]{2,1,0:T(1,128)}), f32[16,1,4608]{2,1,0:T(1,128)S(1)}, u32[]{:S(2)}, u32[]{:S(2)}) async-start(f32[16,1,4608]{2,1,0:T(1,128)} %bitcast.27), calls=%async_computation | async-start | bytes 589824 | tf_op jit(solution)/shard_map/all_to_all | solution.py:324
  18.4 0.0 copy-done.2
  18.4 1.3 %collective-permute-start = (f32[2,32,128]{2,1,0:T(8,128)S(1)}, f32[2,32,128]{2,1,0:T(8,128)S(1)}, u32[]{:S(2)}, u32[]{:S(2)}) collective-permute-start(f32[2,32,128]{2,1,0:T(8,128)S(1)} %copy-done.2), channel_id=1, source_target_pairs={{0,16},{16,32},{32,48},{48,64},{64,80},{80,96},{96,112},{112,128},... | collective-permute-start | bytes 98312 | tf_op jit(solution)/shard_map/ppermute | solution.py:301
  19.7 1.3 %collective-permute-start.1 = (f32[2,32,128]{2,1,0:T(8,128)S(1)}, f32[2,32,128]{2,1,0:T(8,128)S(1)}, u32[]{:S(2)}, u32[]{:S(2)}) collective-permute-start(f32[2,32,128]{2,1,0:T(8,128)S(1)} %copy-done.2), channel_id=1, source_target_pairs={{16,0},{32,16},{48,32},{64,48},{80,64},{96,80},{112,96},{128,112},... | collective-permute-start | bytes 98312 | tf_op jit(solution)/shard_map/ppermute | solution.py:302
  21.0 0.0 copy-done.5
  21.0 0.0 copy-done.4
  21.1 0.0 copy-done.8
  21.1 0.0 copy-done.10
  21.1 0.0 copy-done.7
  21.1 0.0 copy-done.6
  21.1 0.4 plan.1
  21.5 0.0 collective-permute-done.low
  21.5 3.1 %collective-permute-done.1.high = f32[2,32,128]{2,1,0:T(8,128)S(1)} collective-permute-done((f32[2,32,128]{2,1,0:T(8,128)S(1)}, f32[2,32,128]{2,1,0:T(8,128)S(1)}, u32[]{:S(2)}, u32[]{:S(2)}) %collective-permute-start.1) | collective-permute-done | bytes 32800 | tf_op jit(solution)/shard_map/ppermute | solution.py:302
  24.6 0.0 copy-done.9
  24.6 1.4 %copy-done.1 = f32[2,32,6,8,128]{4,3,2,1,0:T(8,128)S(1)} copy-done((f32[2,32,6,8,128]{4,3,2,1,0:T(8,128)S(1)}, f32[2,32,6,8,128]{4,3,2,1,0:T(8,128)}, u32[]{:S(2)}) %copy-start.1) | copy-done | bytes 1572888
  26.0 0.9 %near.1 = f32[2,32,8,128]{3,2,1,0:T(8,128)S(1)} custom-call(s32[6,32]{1,0:T(8,128)S(1)} %bitcast.25, s32[32]{0:T(128)S(1)} %copy-done.11, f32[2,32,128]{2,1,0:T(8,128)S(1)} %collective-permute-done.low, f32[2,32,128]{2,1,0:T(8,128)S(1)} %copy-done.2, f32[2,32,128]{2,1,0:T(8,128)S(1)} %collective-permute-done.1.high, f32[2,32,6,8,128]{4,3,2,1,0:T(8,128)S(1)} %copy-done.1), custom_call_target="tpu_custom_call" | custom-call | flops 4000000 | bytes 4000000 | tf_op jit(solution)/shard_map/near/pallas_call | solution.py:342
  26.9 10.3 %all-to-all-done = f32[16,1,4608]{2,1,0:T(1,128)S(1)} async-done(((f32[16,1,4608]{2,1,0:T(1,128)}), f32[16,1,4608]{2,1,0:T(1,128)S(1)}, u32[]{:S(2)}, u32[]{:S(2)}) %all-to-all-start) | async-done | bytes 294944 | tf_op jit(solution)/shard_map/all_to_all | solution.py:324
  37.2 0.3 lift.1
  37.5 17.8 %all_to_all.15 = f32[32,1,3328]{2,1,0:T(1,128)S(1)} all-to-all(f32[32,1,3328]{2,1,0:T(1,128)S(1)} %bitcast.15), channel_id=1, replica_groups=mesh['box'=32,'dir'=16] {'box'}, dimensions={0} | all-to-all | bytes 851968 | tf_op jit(solution)/shard_map/all_to_all | solution.py:362
  55.3 0.3 lower.1
  55.6 20.5 %all_to_all.16 = f32[16,1,2048]{2,1,0:T(1,128)S(1)} all-to-all(f32[16,1,2048]{2,1,0:T(1,128)S(1)} %bitcast.18), channel_id=1, replica_groups=mesh['box'=32,'dir'=16] {'dir'}, dimensions={0} | all-to-all | bytes 262144 | tf_op jit(solution)/shard_map/all_to_all | solution.py:374
  76.1 0.0 copy-done
  76.1 1.9 %field.1 = f32[2,8,32]{2,1,0:T(8,128)} custom-call(f32[256,128]{1,0:T(8,128)S(1)} %bitcast.17, f32[832,128]{1,0:T(8,128)S(1)} %bitcast.14, f32[2,2,32,8,512]{4,3,2,1,0:T(8,128)S(1)} %copy-done, f32[2,32,8,128]{3,2,1,0:T(8,128)S(1)} %near.1), custom_call_target="tpu_custom_call" | custom-call | tf_op jit(solution)/shard_map/field/pallas_call | solution.py:376
  (14 shorter events, 0.0 us)
Async XLA Ops:
  0.0 18.4 %copy-start.2 = (f32[2,32,128]{2,1,0:T(8,128)S(1)}, f32[2,32,128]{2,1,0:T(8,128)}, u32[]{:S(2)}) copy-start(f32[2,32,128]{2,1,0:T(8,128)} %current.3) | copy-start | bytes 98308
  0.0 21.0 %copy-start.5 = (f32[128,4]{0,1:T(4,128)S(1)}, f32[128,4]{0,1:T(4,128)}, u32[]{:S(2)}) copy-start(f32[128,4]{0,1:T(4,128)} %param.18) | copy-start | bytes 6148
  0.0 21.0 %copy-start.4 = (s32[128,4]{0,1:T(4,128)S(1)}, s32[128,4]{0,1:T(4,128)}, u32[]{:S(2)}) copy-start(s32[128,4]{0,1:T(4,128)} %param.17) | copy-start | bytes 6148
  0.0 21.0 %copy-start.8 = (f32[2,8,128]{2,1,0:T(8,128)S(1)}, f32[2,8,128]{2,1,0:T(8,128)}, u32[]{:S(2)}) copy-start(f32[2,8,128]{2,1,0:T(8,128)} %translation.1) | copy-start | bytes 24580
  0.0 21.0 %copy-start.10 = (s32[128]{0:T(128)S(1)}, s32[128]{0:T(128)}, u32[]{:S(2)}) copy-start(s32[128]{0:T(128)} %param.22) | copy-start | bytes 1540
  0.0 21.0 %copy-start.7 = (s32[128,16]{0,1:T(8,128)S(1)}, s32[128,16]{0,1:T(8,128)}, u32[]{:S(2)}) copy-start(s32[128,16]{0,1:T(8,128)} %param.21) | copy-start | bytes 24580
  0.0 21.0 %copy-start.6 = (s32[128,16]{0,1:T(8,128)S(1)}, s32[128,16]{0,1:T(8,128)}, u32[]{:S(2)}) copy-start(s32[128,16]{0,1:T(8,128)} %param.20) | copy-start | bytes 24580
  0.0 24.5 %copy-start.11 = (s32[32]{0:T(128)S(1)}, s32[32]{0:T(128)}, u32[]{:S(2)}) copy-start(s32[32]{0:T(128)} %near_count.1) | copy-start | bytes 388
  0.1 24.5 %copy-start.9 = (s32[32,6]{0,1:T(8,128)S(1)}, s32[32,6]{0,1:T(8,128)}, u32[]{:S(2)}) copy-start(s32[32,6]{0,1:T(8,128)} %param.14) | copy-start | bytes 2308
  0.1 37.1 %copy-start.3 = (f32[2,8,128]{2,1,0:T(8,128)S(1)}, f32[2,8,128]{2,1,0:T(8,128)}, u32[]{:S(2)}) copy-start(f32[2,8,128]{2,1,0:T(8,128)} %shift.3) | copy-start | bytes 24580
  3.2 34.0 %all-to-all-start = ((f32[16,1,4608]{2,1,0:T(1,128)}), f32[16,1,4608]{2,1,0:T(1,128)S(1)}, u32[]{:S(2)}, u32[]{:S(2)}) async-start(f32[16,1,4608]{2,1,0:T(1,128)} %bitcast.27), calls=%async_computation | async-start | bytes 589824 | tf_op jit(solution)/shard_map/all_to_all | solution.py:324
  18.4 3.1 %collective-permute-start = (f32[2,32,128]{2,1,0:T(8,128)S(1)}, f32[2,32,128]{2,1,0:T(8,128)S(1)}, u32[]{:S(2)}, u32[]{:S(2)}) collective-permute-start(f32[2,32,128]{2,1,0:T(8,128)S(1)} %copy-done.2), channel_id=1, source_target_pairs={{0,16},{16,32},{32,48},{48,64},{64,80},{80,96},{96,112},{112,128},... | collective-permute-start | bytes 98312 | tf_op jit(solution)/shard_map/ppermute | solution.py:301
  19.7 4.8 %collective-permute-start.1 = (f32[2,32,128]{2,1,0:T(8,128)S(1)}, f32[2,32,128]{2,1,0:T(8,128)S(1)}, u32[]{:S(2)}, u32[]{:S(2)}) collective-permute-start(f32[2,32,128]{2,1,0:T(8,128)S(1)} %copy-done.2), channel_id=1, source_target_pairs={{16,0},{32,16},{48,32},{64,48},{80,64},{96,80},{112,96},{128,112},... | collective-permute-start | bytes 98312 | tf_op jit(solution)/shard_map/ppermute | solution.py:302
  24.6 1.4 %copy-start.1 = (f32[2,32,6,8,128]{4,3,2,1,0:T(8,128)S(1)}, f32[2,32,6,8,128]{4,3,2,1,0:T(8,128)}, u32[]{:S(2)}) copy-start(f32[2,32,6,8,128]{4,3,2,1,0:T(8,128)} %blocks.1) | copy-start | bytes 4718596
  26.0 50.1 %copy-start = (f32[2,2,32,8,512]{4,3,2,1,0:T(8,128)S(1)}, f32[2,2,32,8,512]{4,3,2,1,0:T(8,128)}, u32[]{:S(2)}) copy-start(f32[2,2,32,8,512]{4,3,2,1,0:T(8,128)} %radiation.3) | copy-start | bytes 6291460

commit v4 on v3

--- a/solution.py
+++ b/solution.py
@@ -18,6 +18,17 @@
 HBM = pl.BlockSpec(memory_space=pltpu.HBM)
 params = pltpu.CompilerParams(vmem_limit_bytes=12 * 2**20)
 alone = pltpu.CompilerParams(vmem_limit_bytes=60 * 2**20)
+
+
+def sums_of_eight(tiles):
+    row = lax.broadcasted_iota(jnp.int32, tiles[0].shape, 0)
+    for step in (1, 2, 4):
+        even = (row & step) == 0
+        tiles = [
+            jnp.where(even, a, b) + pltpu.roll(jnp.where(even, b, a), 8 - step, 0)
+            for a, b in zip(tiles[0::2], tiles[1::2])
+        ]
+    return tiles[0]
 
 
 def leaf_kernel(cuts, shares, total, spare, current, stencil, weight, shift, radiation, out, patterns, *scratch):
@@ -58,14 +69,20 @@
     real, imag = columns[0, mine, :], columns[1, mine, :]
     for cut in range(cuts):
         copies[cut].wait()
-        for box in range(cut * step, (cut + 1) * step):
-            cur_re, cur_im = real[:, box : box + 1], imag[:, box : box + 1]
+        for group in range(cut * step, (cut + 1) * step, 8):
+            eight = range(group, group + 8)
+            cur_re = [jnp.broadcast_to(real[:, box : box + 1], (own, 128)) for box in eight]
+            cur_im = [jnp.broadcast_to(imag[:, box : box + 1], (own, 128)) for box in eight]
             for pol in range(pols):
-                rad_re, rad_im = patterns[0, pol, box], patterns[1, pol, box]
-                at = pol * boxes + box
-                rows[at : at + 1, :] = jnp.sum(rad_re * cur_re - rad_im * cur_im, axis=0, keepdims=True)
-                at = (pols + pol) * boxes + box
-                rows[at : at + 1, :] = jnp.sum(rad_re * cur_im + rad_im * cur_re, axis=0, keepdims=True)
+                for block in range(width // 128):
+                    at = slice(block * 128, block * 128 + 128)
+                    rad_re = [patterns[0, pol, box, :, at] for box in eight]
+                    rad_im = [patterns[1, pol, box, :, at] for box in eight]
+                    both = list(zip(rad_re, rad_im, cur_re, cur_im))
+                    line = pol * boxes + group
+                    rows[line : line + 8, at] = sums_of_eight([a * c - b * d for a, b, c, d in both])
+                    line = (pols + pol) * boxes + group
+                    rows[line : line + 8, at] = sums_of_eight([a * d + b * c for a, b, c, d in both])
     for block in range(width // 128):
         samples[lead + block * 128 : lead + block * 128 + 128, :] = rows[:, block * 128 : block * 128 + 128].T
     samples[lead - below : lead, :] = samples[lead + width - below : lead + width, :]

time: 78.4 us -> 78.1 us (level)
  no operation moved by 1% of the time
where the time goes in v4:
time: 78.1 us; the launch traced here: 77.8 us
  blocking collectives  38.3 us (49%)
  starting transfers between devices  17.8 us (23%)
  waiting for transfers between devices  13.4 us (17%)
  Pallas kernels  6.63 us (8%)
  local copies, waits for them, and re-layouts  1.45 us (2%)
    all_to_all x1, blocking collectives, local(): lax.all_to_all(moved.reshape(dir_total, 1, lanes // 8 * share), 'dir', 0,...  20.5 us
    all_to_all x1, blocking collectives, local(): lax.all_to_all(tops.reshape(box_total, 1, height * share), 'box', 0, 0, t...  17.8 us
    all_to_all x1, starting transfers between devices, local(): lax.all_to_all(windows.reshape(dir_total, 1, (span + spare) * lanes), 'di...  15.2 us
    all_to_all x1, waiting for transfers between devices, local(): lax.all_to_all(windows.reshape(dir_total, 1, (span + spare) * lanes), 'di...  10.3 us
    ppermute x1, waiting for transfers between devices, local(): high = lax.ppermute(current, 'box', [(b, a) for a, b in forward])  3.06 us
    pallas_call x1, Pallas kernels, local(): pl.pallas_call(functools.partial(leaf_kernel, cuts, dir_total, box_total,...  2.81 us
    pallas_call x1, Pallas kernels, local(): pl.pallas_call(functools.partial(field_kernel, dir_total, box_total), out...  1.94 us
  transfers between devices with their start and end apart: 3, of which 2 were waited for; matrix products, arithmetic and copies ran while one was open for 0% of the time, Pallas kernels for 2%

profile of v4, /device:TPU:32, one launch (start us, length us, event | category | flops | bytes accessed | tf_op | source)
XLA Modules:
  0.0 77.8 jit_solution(4493833950216938207)
XLA Ops:
  0.0 0.0 copy-start.8
  0.0 0.0 copy-start.10
  0.1 2.8 %leaf.1 = f32[576,128]{1,0:T(8,128)} custom-call(f32[2,32,128]{2,1,0:T(8,128)} %current.3, s32[4,128]{1,0:T(4,128)} %bitcast.19, f32[4,128]{1,0:T(4,128)} %bitcast.21, f32[2,8,128]{2,1,0:T(8,128)} %shift.3, f32[2,2,32,8,512]{4,3,2,1,0:T(8,128)} %radiation.3), custom_call_target="tpu_custom_call" | custom-call | tf_op jit(solution)/shard_map/leaf/pallas_call | solution.py:321
  2.9 15.2 %all-to-all-start = ((f32[16,1,4608]{2,1,0:T(1,128)}), f32[16,1,4608]{2,1,0:T(1,128)S(1)}, u32[]{:S(2)}, u32[]{:S(2)}) async-start(f32[16,1,4608]{2,1,0:T(1,128)} %bitcast.27), calls=%async_computation | async-start | bytes 589824 | tf_op jit(solution)/shard_map/all_to_all | solution.py:341
  18.1 1.3 %collective-permute-start = (f32[2,32,128]{2,1,0:T(8,128)S(1)}, f32[2,32,128]{2,1,0:T(8,128)S(1)}, u32[]{:S(2)}, u32[]{:S(2)}) collective-permute-start(f32[2,32,128]{2,1,0:T(8,128)S(1)} %copy-done.2), channel_id=1, source_target_pairs={{0,16},{16,32},{32,48},{48,64},{64,80},{80,96},{96,112},{112,128},... | collective-permute-start | bytes 98312 | tf_op jit(solution)/shard_map/ppermute | solution.py:318
  19.4 1.3 %collective-permute-start.1 = (f32[2,32,128]{2,1,0:T(8,128)S(1)}, f32[2,32,128]{2,1,0:T(8,128)S(1)}, u32[]{:S(2)}, u32[]{:S(2)}) collective-permute-start(f32[2,32,128]{2,1,0:T(8,128)S(1)} %copy-done.2), channel_id=1, source_target_pairs={{16,0},{32,16},{48,32},{64,48},{80,64},{96,80},{112,96},{128,112},... | collective-permute-start | bytes 98312 | tf_op jit(solution)/shard_map/ppermute | solution.py:319
  20.7 0.0 copy-done.5
  20.7 0.0 copy-done.4
  20.7 0.0 copy-done.8
  20.8 0.0 copy-done.10
  20.8 0.0 copy-done.7
  20.8 0.0 copy-done.6
  20.8 0.4 plan.1
  21.2 0.0 collective-permute-done.low
  21.2 3.1 %collective-permute-done.1.high = f32[2,32,128]{2,1,0:T(8,128)S(1)} collective-permute-done((f32[2,32,128]{2,1,0:T(8,128)S(1)}, f32[2,32,128]{2,1,0:T(8,128)S(1)}, u32[]{:S(2)}, u32[]{:S(2)}) %collective-permute-start.1) | collective-permute-done | bytes 32800 | tf_op jit(solution)/shard_map/ppermute | solution.py:319
  24.3 0.0 copy-done.9
  24.3 1.4 %copy-done.1 = f32[2,32,6,8,128]{4,3,2,1,0:T(8,128)S(1)} copy-done((f32[2,32,6,8,128]{4,3,2,1,0:T(8,128)S(1)}, f32[2,32,6,8,128]{4,3,2,1,0:T(8,128)}, u32[]{:S(2)}) %copy-start.1) | copy-done | bytes 1572888
  25.7 0.9 %near.1 = f32[2,32,8,128]{3,2,1,0:T(8,128)S(1)} custom-call(s32[6,32]{1,0:T(8,128)S(1)} %bitcast.25, s32[32]{0:T(128)S(1)} %copy-done.11, f32[2,32,128]{2,1,0:T(8,128)S(1)} %collective-permute-done.low, f32[2,32,128]{2,1,0:T(8,128)S(1)} %copy-done.2, f32[2,32,128]{2,1,0:T(8,128)S(1)} %collective-permute-done.1.high, f32[2,32,6,8,128]{4,3,2,1,0:T(8,128)S(1)} %copy-done.1), custom_call_target="tpu_custom_call" | custom-call | flops 4000000 | bytes 4000000 | tf_op jit(solution)/shard_map/near/pallas_call | solution.py:359
  26.6 10.3 %all-to-all-done = f32[16,1,4608]{2,1,0:T(1,128)S(1)} async-done(((f32[16,1,4608]{2,1,0:T(1,128)}), f32[16,1,4608]{2,1,0:T(1,128)S(1)}, u32[]{:S(2)}, u32[]{:S(2)}) %all-to-all-start) | async-done | bytes 294944 | tf_op jit(solution)/shard_map/all_to_all | solution.py:341
  36.9 0.3 lift.1
  37.2 17.8 %all_to_all.15 = f32[32,1,3328]{2,1,0:T(1,128)S(1)} all-to-all(f32[32,1,3328]{2,1,0:T(1,128)S(1)} %bitcast.15), channel_id=1, replica_groups=mesh['box'=32,'dir'=16] {'box'}, dimensions={0} | all-to-all | bytes 851968 | tf_op jit(solution)/shard_map/all_to_all | solution.py:379
  55.0 0.3 lower.1
  55.3 20.5 %all_to_all.16 = f32[16,1,2048]{2,1,0:T(1,128)S(1)} all-to-all(f32[16,1,2048]{2,1,0:T(1,128)S(1)} %bitcast.18), channel_id=1, replica_groups=mesh['box'=32,'dir'=16] {'dir'}, dimensions={0} | all-to-all | bytes 262144 | tf_op jit(solution)/shard_map/all_to_all | solution.py:391
  75.8 1.9 %field.1 = f32[2,8,32]{2,1,0:T(8,128)} custom-call(f32[256,128]{1,0:T(8,128)S(1)} %bitcast.17, f32[832,128]{1,0:T(8,128)S(1)} %bitcast.14, f32[2,2,32,8,512]{4,3,2,1,0:T(8,128)S(1)} %copy-done, f32[2,32,8,128]{3,2,1,0:T(8,128)S(1)} %near.1), custom_call_target="tpu_custom_call" | custom-call | tf_op jit(solution)/shard_map/field/pallas_call | solution.py:393
  (14 shorter events, 0.0 us)
Async XLA Ops:
  0.0 18.1 %copy-start.2 = (f32[2,32,128]{2,1,0:T(8,128)S(1)}, f32[2,32,128]{2,1,0:T(8,128)}, u32[]{:S(2)}) copy-start(f32[2,32,128]{2,1,0:T(8,128)} %current.3) | copy-start | bytes 98308
  0.0 20.7 %copy-start.5 = (f32[128,4]{0,1:T(4,128)S(1)}, f32[128,4]{0,1:T(4,128)}, u32[]{:S(2)}) copy-start(f32[128,4]{0,1:T(4,128)} %param.18) | copy-start | bytes 6148
  0.0 20.7 %copy-start.4 = (s32[128,4]{0,1:T(4,128)S(1)}, s32[128,4]{0,1:T(4,128)}, u32[]{:S(2)}) copy-start(s32[128,4]{0,1:T(4,128)} %param.17) | copy-start | bytes 6148
  0.0 20.7 %copy-start.8 = (f32[2,8,128]{2,1,0:T(8,128)S(1)}, f32[2,8,128]{2,1,0:T(8,128)}, u32[]{:S(2)}) copy-start(f32[2,8,128]{2,1,0:T(8,128)} %translation.1) | copy-start | bytes 24580
  0.0 20.7 %copy-start.10 = (s32[128]{0:T(128)S(1)}, s32[128]{0:T(128)}, u32[]{:S(2)}) copy-start(s32[128]{0:T(128)} %param.22) | copy-start | bytes 1540
  0.0 20.7 %copy-start.7 = (s32[128,16]{0,1:T(8,128)S(1)}, s32[128,16]{0,1:T(8,128)}, u32[]{:S(2)}) copy-start(s32[128,16]{0,1:T(8,128)} %param.21) | copy-start | bytes 24580
  0.0 20.7 %copy-start.6 = (s32[128,16]{0,1:T(8,128)S(1)}, s32[128,16]{0,1:T(8,128)}, u32[]{:S(2)}) copy-start(s32[128,16]{0,1:T(8,128)} %param.20) | copy-start | bytes 24580
  0.0 24.2 %copy-start.11 = (s32[32]{0:T(128)S(1)}, s32[32]{0:T(128)}, u32[]{:S(2)}) copy-start(s32[32]{0:T(128)} %near_count.1) | copy-start | bytes 388
  0.1 24.2 %copy-start.9 = (s32[32,6]{0,1:T(8,128)S(1)}, s32[32,6]{0,1:T(8,128)}, u32[]{:S(2)}) copy-start(s32[32,6]{0,1:T(8,128)} %param.14) | copy-start | bytes 2308
  0.1 36.8 %copy-start.3 = (f32[2,8,128]{2,1,0:T(8,128)S(1)}, f32[2,8,128]{2,1,0:T(8,128)}, u32[]{:S(2)}) copy-start(f32[2,8,128]{2,1,0:T(8,128)} %shift.3) | copy-start | bytes 24580
  2.9 34.0 %all-to-all-start = ((f32[16,1,4608]{2,1,0:T(1,128)}), f32[16,1,4608]{2,1,0:T(1,128)S(1)}, u32[]{:S(2)}, u32[]{:S(2)}) async-start(f32[16,1,4608]{2,1,0:T(1,128)} %bitcast.27), calls=%async_computation | async-start | bytes 589824 | tf_op jit(solution)/shard_map/all_to_all | solution.py:341
  18.1 3.1 %collective-permute-start = (f32[2,32,128]{2,1,0:T(8,128)S(1)}, f32[2,32,128]{2,1,0:T(8,128)S(1)}, u32[]{:S(2)}, u32[]{:S(2)}) collective-permute-start(f32[2,32,128]{2,1,0:T(8,128)S(1)} %copy-done.2), channel_id=1, source_target_pairs={{0,16},{16,32},{32,48},{48,64},{64,80},{80,96},{96,112},{112,128},... | collective-permute-start | bytes 98312 | tf_op jit(solution)/shard_map/ppermute | solution.py:318
  19.4 4.8 %collective-permute-start.1 = (f32[2,32,128]{2,1,0:T(8,128)S(1)}, f32[2,32,128]{2,1,0:T(8,128)S(1)}, u32[]{:S(2)}, u32[]{:S(2)}) collective-permute-start(f32[2,32,128]{2,1,0:T(8,128)S(1)} %copy-done.2), channel_id=1, source_target_pairs={{16,0},{32,16},{48,32},{64,48},{80,64},{96,80},{112,96},{128,112},... | collective-permute-start | bytes 98312 | tf_op jit(solution)/shard_map/ppermute | solution.py:319
  24.3 1.4 %copy-start.1 = (f32[2,32,6,8,128]{4,3,2,1,0:T(8,128)S(1)}, f32[2,32,6,8,128]{4,3,2,1,0:T(8,128)}, u32[]{:S(2)}) copy-start(f32[2,32,6,8,128]{4,3,2,1,0:T(8,128)} %blocks.1) | copy-start | bytes 4718596
  25.7 50.2 %copy-start = (f32[2,2,32,8,512]{4,3,2,1,0:T(8,128)S(1)}, f32[2,2,32,8,512]{4,3,2,1,0:T(8,128)}, u32[]{:S(2)}) copy-start(f32[2,2,32,8,512]{4,3,2,1,0:T(8,128)} %radiation.3) | copy-start | bytes 6291460

commit v5 on v4

--- a/solution.py
+++ b/solution.py
@@ -11,6 +11,7 @@
 f32 = jnp.float32
 below, above = 1, 2
 lead = 8
+tall_window = 48
 reach = below + above + 1
 VMEM = pl.BlockSpec(memory_space=pltpu.VMEM)
 SMEM = pl.BlockSpec(memory_space=pltpu.SMEM)
@@ -234,13 +235,13 @@
         return parts[0] if len(parts) == 1 else jnp.concatenate(parts, axis=0)
 
     samples[...] = jnp.zeros_like(samples)
-    sample = lax.broadcasted_iota(jnp.int32, (40, lanes), 0)
-    offset = sample - lax.broadcasted_iota(jnp.int32, (40, lanes), 1) // (lanes // piece)
+    sample = lax.broadcasted_iota(jnp.int32, (tall_window, lanes), 0)
+    offset = sample - lax.broadcasted_iota(jnp.int32, (tall_window, lanes), 1) // (lanes // piece)
     contract = (((1,), (1,)), ((), ()))
     for share in range(shares):
         number = share * (16 + reach)
         shift_re, shift_im = octants(number), octants(number + 8)
-        table = jnp.zeros((40, lanes), f32)
+        table = jnp.zeros((tall_window, lanes), f32)
         for step in range(reach):
             at = table_row(number + 16 + step)
             table = jnp.where(offset == step, gathered[at : at + 1, :], table)
@@ -254,14 +255,16 @@
         value_lo = (value - value_hi.astype(f32)).astype(jnp.bfloat16)
         table_hi = table.astype(jnp.bfloat16)
         table_lo = (table - table_hi.astype(f32)).astype(jnp.bfloat16)
-        settled = lax.dot_general(
-            jnp.concatenate([table_hi, table_hi], axis=1),
+        tables = jnp.concatenate([table_hi, table_lo], axis=0)
+        both = lax.dot_general(
+            jnp.concatenate([tables, tables], axis=1),
             jnp.concatenate([value_hi, value_lo], axis=1),
             contract,
             preferred_element_type=f32,
-        ) + lax.dot_general(table_lo, value_hi, contract, preferred_element_type=f32)
+        )
+        settled = both[:tall_window] + both[tall_window:]
         first = lead - below + share * piece
-        samples[first : first + 40, :] += settled
+        samples[first : first + tall_window, :] += settled
     samples[lead + width - below : lead + width, :] += samples[lead - below : lead, :]
     samples[lead : lead + above, :] += samples[lead + width : lead + width + above, :]
     for block in range(width // 128):
@@ -306,7 +309,7 @@
     piece = width // dir_total
     span = piece + below + above
     lanes = 2 * pols * boxes
-    held = lead + width + 8
+    held = lead + width + 16
     cuts = 4
     spare = -(-(16 + reach) // box_total)
     height = lanes // 8 + (16 + reach) * dir_total // box_total

time: 78.1 us -> 77.8 us (level)
  no operation moved by 1% of the time
where the time goes in v5:
time: 77.8 us; the launch traced here: 77.4 us
  blocking collectives  38.3 us (49%)
  starting transfers between devices  17.8 us (23%)
  waiting for transfers between devices  13.4 us (17%)
  Pallas kernels  6.33 us (8%)
  local copies, waits for them, and re-layouts  1.45 us (2%)
    all_to_all x1, blocking collectives, local(): lax.all_to_all(moved.reshape(dir_total, 1, lanes // 8 * share), 'dir', 0,...  20.5 us
    all_to_all x1, blocking collectives, local(): lax.all_to_all(tops.reshape(box_total, 1, height * share), 'box', 0, 0, t...  17.8 us
    all_to_all x1, starting transfers between devices, local(): lax.all_to_all(windows.reshape(dir_total, 1, (span + spare) * lanes), 'di...  15.2 us
    all_to_all x1, waiting for transfers between devices, local(): lax.all_to_all(windows.reshape(dir_total, 1, (span + spare) * lanes), 'di...  10.3 us
    ppermute x1, waiting for transfers between devices, local(): high = lax.ppermute(current, 'box', [(b, a) for a, b in forward])  3.06 us
    pallas_call x1, Pallas kernels, local(): pl.pallas_call(functools.partial(leaf_kernel, cuts, dir_total, box_total,...  2.81 us
    pallas_call x1, Pallas kernels, local(): pl.pallas_call(functools.partial(field_kernel, dir_total, box_total), out...  1.63 us
  transfers between devices with their start and end apart: 3, of which 2 were waited for; matrix products, arithmetic and copies ran while one was open for 0% of the time, Pallas kernels for 2%

profile of v5, /device:TPU:32, one launch (start us, length us, event | category | flops | bytes accessed | tf_op | source)
XLA Modules:
  0.0 77.4 jit_solution(12742695768922147865)
XLA Ops:
  0.0 0.0 copy-start.8
  0.0 0.0 copy-start.10
  0.0 0.0 copy-start.7
  0.0 0.0 copy-start.6
  0.0 0.0 copy-start.11
  0.1 0.0 copy-start.9
  0.1 0.0 copy-start.3
  0.1 2.8 %leaf.1 = f32[576,128]{1,0:T(8,128)} custom-call(f32[2,32,128]{2,1,0:T(8,128)} %current.3, s32[4,128]{1,0:T(4,128)} %bitcast.19, f32[4,128]{1,0:T(4,128)} %bitcast.21, f32[2,8,128]{2,1,0:T(8,128)} %shift.3, f32[2,2,32,8,512]{4,3,2,1,0:T(8,128)} %radiation.3), custom_call_target="tpu_custom_call" | custom-call | tf_op jit(solution)/shard_map/leaf/pallas_call | solution.py:324
  2.9 15.2 %all-to-all-start = ((f32[16,1,4608]{2,1,0:T(1,128)}), f32[16,1,4608]{2,1,0:T(1,128)S(1)}, u32[]{:S(2)}, u32[]{:S(2)}) async-start(f32[16,1,4608]{2,1,0:T(1,128)} %bitcast.27), calls=%async_computation | async-start | bytes 589824 | tf_op jit(solution)/shard_map/all_to_all | solution.py:344
  18.1 0.0 copy-done.2
  18.1 1.3 %collective-permute-start = (f32[2,32,128]{2,1,0:T(8,128)S(1)}, f32[2,32,128]{2,1,0:T(8,128)S(1)}, u32[]{:S(2)}, u32[]{:S(2)}) collective-permute-start(f32[2,32,128]{2,1,0:T(8,128)S(1)} %copy-done.2), channel_id=1, source_target_pairs={{0,16},{16,32},{32,48},{48,64},{64,80},{80,96},{96,112},{112,128},... | collective-permute-start | bytes 98312 | tf_op jit(solution)/shard_map/ppermute | solution.py:321
  19.4 1.3 %collective-permute-start.1 = (f32[2,32,128]{2,1,0:T(8,128)S(1)}, f32[2,32,128]{2,1,0:T(8,128)S(1)}, u32[]{:S(2)}, u32[]{:S(2)}) collective-permute-start(f32[2,32,128]{2,1,0:T(8,128)S(1)} %copy-done.2), channel_id=1, source_target_pairs={{16,0},{32,16},{48,32},{64,48},{80,64},{96,80},{112,96},{128,112},... | collective-permute-start | bytes 98312 | tf_op jit(solution)/shard_map/ppermute | solution.py:322
  20.8 0.4 plan.1
  21.2 0.0 collective-permute-done.low
  21.2 3.1 %collective-permute-done.1.high = f32[2,32,128]{2,1,0:T(8,128)S(1)} collective-permute-done((f32[2,32,128]{2,1,0:T(8,128)S(1)}, f32[2,32,128]{2,1,0:T(8,128)S(1)}, u32[]{:S(2)}, u32[]{:S(2)}) %collective-permute-start.1) | collective-permute-done | bytes 32800 | tf_op jit(solution)/shard_map/ppermute | solution.py:322
  24.3 1.4 %copy-done.1 = f32[2,32,6,8,128]{4,3,2,1,0:T(8,128)S(1)} copy-done((f32[2,32,6,8,128]{4,3,2,1,0:T(8,128)S(1)}, f32[2,32,6,8,128]{4,3,2,1,0:T(8,128)}, u32[]{:S(2)}) %copy-start.1) | copy-done | bytes 1572888
  25.7 0.9 %near.1 = f32[2,32,8,128]{3,2,1,0:T(8,128)S(1)} custom-call(s32[6,32]{1,0:T(8,128)S(1)} %bitcast.25, s32[32]{0:T(128)S(1)} %copy-done.11, f32[2,32,128]{2,1,0:T(8,128)S(1)} %collective-permute-done.low, f32[2,32,128]{2,1,0:T(8,128)S(1)} %copy-done.2, f32[2,32,128]{2,1,0:T(8,128)S(1)} %collective-permute-done.1.high, f32[2,32,6,8,128]{4,3,2,1,0:T(8,128)S(1)} %copy-done.1), custom_call_target="tpu_custom_call" | custom-call | flops 4000000 | bytes 4000000 | tf_op jit(solution)/shard_map/near/pallas_call | solution.py:362
  26.6 10.3 %all-to-all-done = f32[16,1,4608]{2,1,0:T(1,128)S(1)} async-done(((f32[16,1,4608]{2,1,0:T(1,128)}), f32[16,1,4608]{2,1,0:T(1,128)S(1)}, u32[]{:S(2)}, u32[]{:S(2)}) %all-to-all-start) | async-done | bytes 294944 | tf_op jit(solution)/shard_map/all_to_all | solution.py:344
  36.9 0.0 copy-done.3
  36.9 0.3 lift.1
  37.2 17.8 %all_to_all.15 = f32[32,1,3328]{2,1,0:T(1,128)S(1)} all-to-all(f32[32,1,3328]{2,1,0:T(1,128)S(1)} %bitcast.15), channel_id=1, replica_groups=mesh['box'=32,'dir'=16] {'box'}, dimensions={0} | all-to-all | bytes 851968 | tf_op jit(solution)/shard_map/all_to_all | solution.py:382
  55.0 0.3 lower.1
  55.3 20.5 %all_to_all.16 = f32[16,1,2048]{2,1,0:T(1,128)S(1)} all-to-all(f32[16,1,2048]{2,1,0:T(1,128)S(1)} %bitcast.18), channel_id=1, replica_groups=mesh['box'=32,'dir'=16] {'dir'}, dimensions={0} | all-to-all | bytes 262144 | tf_op jit(solution)/shard_map/all_to_all | solution.py:394
  75.8 1.6 %field.1 = f32[2,8,32]{2,1,0:T(8,128)} custom-call(f32[256,128]{1,0:T(8,128)S(1)} %bitcast.17, f32[832,128]{1,0:T(8,128)S(1)} %bitcast.14, f32[2,2,32,8,512]{4,3,2,1,0:T(8,128)S(1)} %copy-done, f32[2,32,8,128]{3,2,1,0:T(8,128)S(1)} %near.1), custom_call_target="tpu_custom_call" | custom-call | tf_op jit(solution)/shard_map/field/pallas_call | solution.py:396
  (14 shorter events, 0.0 us)
Async XLA Ops:
  0.0 18.1 %copy-start.2 = (f32[2,32,128]{2,1,0:T(8,128)S(1)}, f32[2,32,128]{2,1,0:T(8,128)}, u32[]{:S(2)}) copy-start(f32[2,32,128]{2,1,0:T(8,128)} %current.3) | copy-start | bytes 98308
  0.0 20.7 %copy-start.5 = (f32[128,4]{0,1:T(4,128)S(1)}, f32[128,4]{0,1:T(4,128)}, u32[]{:S(2)}) copy-start(f32[128,4]{0,1:T(4,128)} %param.18) | copy-start | bytes 6148
  0.0 20.7 %copy-start.4 = (s32[128,4]{0,1:T(4,128)S(1)}, s32[128,4]{0,1:T(4,128)}, u32[]{:S(2)}) copy-start(s32[128,4]{0,1:T(4,128)} %param.17) | copy-start | bytes 6148
  0.0 20.7 %copy-start.8 = (f32[2,8,128]{2,1,0:T(8,128)S(1)}, f32[2,8,128]{2,1,0:T(8,128)}, u32[]{:S(2)}) copy-start(f32[2,8,128]{2,1,0:T(8,128)} %translation.1) | copy-start | bytes 24580
  0.0 20.7 %copy-start.10 = (s32[128]{0:T(128)S(1)}, s32[128]{0:T(128)}, u32[]{:S(2)}) copy-start(s32[128]{0:T(128)} %param.22) | copy-start | bytes 1540
  0.0 20.7 %copy-start.7 = (s32[128,16]{0,1:T(8,128)S(1)}, s32[128,16]{0,1:T(8,128)}, u32[]{:S(2)}) copy-start(s32[128,16]{0,1:T(8,128)} %param.21) | copy-start | bytes 24580
  0.0 20.7 %copy-start.6 = (s32[128,16]{0,1:T(8,128)S(1)}, s32[128,16]{0,1:T(8,128)}, u32[]{:S(2)}) copy-start(s32[128,16]{0,1:T(8,128)} %param.20) | copy-start | bytes 24580
  0.0 24.2 %copy-start.11 = (s32[32]{0:T(128)S(1)}, s32[32]{0:T(128)}, u32[]{:S(2)}) copy-start(s32[32]{0:T(128)} %near_count.1) | copy-start | bytes 388
  0.1 24.2 %copy-start.9 = (s32[32,6]{0,1:T(8,128)S(1)}, s32[32,6]{0,1:T(8,128)}, u32[]{:S(2)}) copy-start(s32[32,6]{0,1:T(8,128)} %param.14) | copy-start | bytes 2308
  0.1 36.8 %copy-start.3 = (f32[2,8,128]{2,1,0:T(8,128)S(1)}, f32[2,8,128]{2,1,0:T(8,128)}, u32[]{:S(2)}) copy-start(f32[2,8,128]{2,1,0:T(8,128)} %shift.3) | copy-start | bytes 24580
  2.9 34.0 %all-to-all-start = ((f32[16,1,4608]{2,1,0:T(1,128)}), f32[16,1,4608]{2,1,0:T(1,128)S(1)}, u32[]{:S(2)}, u32[]{:S(2)}) async-start(f32[16,1,4608]{2,1,0:T(1,128)} %bitcast.27), calls=%async_computation | async-start | bytes 589824 | tf_op jit(solution)/shard_map/all_to_all | solution.py:344
  18.1 3.1 %collective-permute-start = (f32[2,32,128]{2,1,0:T(8,128)S(1)}, f32[2,32,128]{2,1,0:T(8,128)S(1)}, u32[]{:S(2)}, u32[]{:S(2)}) collective-permute-start(f32[2,32,128]{2,1,0:T(8,128)S(1)} %copy-done.2), channel_id=1, source_target_pairs={{0,16},{16,32},{32,48},{48,64},{64,80},{80,96},{96,112},{112,128},... | collective-permute-start | bytes 98312 | tf_op jit(solution)/shard_map/ppermute | solution.py:321
  19.4 4.8 %collective-permute-start.1 = (f32[2,32,128]{2,1,0:T(8,128)S(1)}, f32[2,32,128]{2,1,0:T(8,128)S(1)}, u32[]{:S(2)}, u32[]{:S(2)}) collective-permute-start(f32[2,32,128]{2,1,0:T(8,128)S(1)} %copy-done.2), channel_id=1, source_target_pairs={{16,0},{32,16},{48,32},{64,48},{80,64},{96,80},{112,96},{128,112},... | collective-permute-start | bytes 98312 | tf_op jit(solution)/shard_map/ppermute | solution.py:322
  24.3 1.4 %copy-start.1 = (f32[2,32,6,8,128]{4,3,2,1,0:T(8,128)S(1)}, f32[2,32,6,8,128]{4,3,2,1,0:T(8,128)}, u32[]{:S(2)}) copy-start(f32[2,32,6,8,128]{4,3,2,1,0:T(8,128)} %blocks.1) | copy-start | bytes 4718596
  25.7 50.1 %copy-start = (f32[2,2,32,8,512]{4,3,2,1,0:T(8,128)S(1)}, f32[2,2,32,8,512]{4,3,2,1,0:T(8,128)}, u32[]{:S(2)}) copy-start(f32[2,2,32,8,512]{4,3,2,1,0:T(8,128)} %radiation.3) | copy-start | bytes 6291460

commit v6 on v5

--- a/solution.py
+++ b/solution.py
@@ -15,7 +15,6 @@
 reach = below + above + 1
 VMEM = pl.BlockSpec(memory_space=pltpu.VMEM)
 SMEM = pl.BlockSpec(memory_space=pltpu.SMEM)
-ANY = pl.BlockSpec(memory_space=pl.ANY)
 HBM = pl.BlockSpec(memory_space=pltpu.HBM)
 params = pltpu.CompilerParams(vmem_limit_bytes=12 * 2**20)
 alone = pltpu.CompilerParams(vmem_limit_bytes=60 * 2**20)
@@ -128,7 +127,7 @@
             factors[part, which * parents : (which + 1) * parents, :] = jnp.broadcast_to(one, (parents, lanes))
 
 
-def lift_kernel(shares, copies, spare, received, interp, shift, near, out, total, tops):
+def lift_kernel(shares, copies, spare, received, interp, shift, out, total, tops):
     each = received.shape[0] // shares
     span = each - spare
     total[...] = jnp.zeros_like(total)
@@ -373,12 +372,12 @@
     tops = pl.pallas_call(
         functools.partial(lift_kernel, dir_total, box_total, spare),
         out_shape=shape((box_total * height, share)),
-        in_specs=[VMEM] * 3 + [ANY],
+        in_specs=[VMEM] * 3,
         out_specs=VMEM,
         scratch_shapes=[pltpu.VMEM((128, lanes), f32), pltpu.VMEM((height, share), f32)],
         compiler_params=params,
         name="lift",
-    )(windows.reshape(dir_total * (span + spare), lanes), interp, child_shift, near)
+    )(windows.reshape(dir_total * (span + spare), lanes), interp, child_shift)
     gathered = lax.all_to_all(tops.reshape(box_total, 1, height * share), "box", 0, 0, tiled=True)
     gathered = gathered.reshape(box_total * height, share)
 

time: 77.8 us -> 79 us (1.015)
  blocking collectives: 38.3 us -> 17.9 us
  waiting for transfers between devices: 13.4 us -> 27.1 us
  starting transfers between devices: 17.8 us -> 24.9 us
    all_to_all x1 -> x0, blocking collectives: 20.5 us -> none  [local(): lax.all_to_all(moved.reshape(dir_total, 1, lanes // 8 * share), 'dir', 0,...]
    all_to_all x1, waiting for transfers between devices: 10.3 us -> 18.3 us  [local(): lax.all_to_all(windows.reshape(dir_total, 1, (span + spare) * lanes), 'di...]
    all_to_all x0 -> x1, starting transfers between devices: none -> 6.8 us  [local(): lax.all_to_all(moved.reshape(dir_total, 1, lanes // 8 * share), 'dir', 0,...]
    all_to_all x0 -> x1, waiting for transfers between devices: none -> 6.37 us  [local(): lax.all_to_all(moved.reshape(dir_total, 1, lanes // 8 * share), 'dir', 0,...]
  transfers between devices with their start and end apart: 3 -> 4, of which waited for: 2 -> 3; matrix products, arithmetic and copies ran while one was open for 0% -> 0% of each run, Pallas kernels for 2% -> 2%
where the time goes in v6:
time: 79 us; the launch traced here: 78.6 us
  waiting for transfers between devices  27.1 us (34%)
  starting transfers between devices  24.9 us (32%)
  blocking collectives  17.9 us (23%)
  Pallas kernels  6.99 us (9%)
  local copies, waits for them, and re-layouts  1.46 us (2%)
    all_to_all x1, waiting for transfers between devices, local(): lax.all_to_all(windows.reshape(dir_total, 1, (span + spare) * lanes), 'di...  18.3 us
    all_to_all x1, blocking collectives, local(): lax.all_to_all(tops.reshape(box_total, 1, height * share), 'box', 0, 0, t...  17.9 us
    all_to_all x1, starting transfers between devices, local(): lax.all_to_all(windows.reshape(dir_total, 1, (span + spare) * lanes), 'di...  15.4 us
    all_to_all x1, starting transfers between devices, local(): lax.all_to_all(moved.reshape(dir_total, 1, lanes // 8 * share), 'dir', 0,...  6.8 us
    all_to_all x1, waiting for transfers between devices, local(): lax.all_to_all(moved.reshape(dir_total, 1, lanes // 8 * share), 'dir', 0,...  6.37 us
    pallas_call x1, Pallas kernels, local(): pl.pallas_call(functools.partial(leaf_kernel, cuts, dir_total, box_total,...  2.81 us
    ppermute x1, waiting for transfers between devices, local(): high = lax.ppermute(current, 'box', [(b, a) for a, b in forward])  2.46 us
    pallas_call x1, Pallas kernels, local(): pl.pallas_call(functools.partial(field_kernel, dir_total, box_total), out...  1.63 us
  transfers between devices with their start and end apart: 4, of which 3 were waited for; matrix products, arithmetic and copies ran while one was open for 0% of the time, Pallas kernels for 2%

profile of v6, /device:TPU:32, one launch (start us, length us, event | category | flops | bytes accessed | tf_op | source)
XLA Modules:
  0.0 78.6 jit_solution(293391182646518223)
XLA Ops:
  0.0 0.0 copy-start.6
  0.0 0.0 copy-start.7
  0.0 0.0 copy-start.10
  0.0 0.0 copy-start.8
  0.0 2.8 %leaf.1 = f32[576,128]{1,0:T(8,128)} custom-call(f32[2,32,128]{2,1,0:T(8,128)} %current.3, s32[4,128]{1,0:T(4,128)} %bitcast.18, f32[4,128]{1,0:T(4,128)} %bitcast.20, f32[2,8,128]{2,1,0:T(8,128)} %shift.3, f32[2,2,32,8,512]{4,3,2,1,0:T(8,128)} %radiation.3), custom_call_target="tpu_custom_call" | custom-call | tf_op jit(solution)/shard_map/leaf/pallas_call | solution.py:323
  2.9 0.0 copy-start.2
  2.9 0.0 copy-start.9
  2.9 0.0 copy-start.11
  2.9 15.4 %all-to-all-start = ((f32[16,1,4608]{2,1,0:T(1,128)}), f32[16,1,4608]{2,1,0:T(1,128)S(1)}, u32[]{:S(2)}, u32[]{:S(2)}) async-start(f32[16,1,4608]{2,1,0:T(1,128)} %bitcast.26), calls=%async_computation | async-start | bytes 589824 | tf_op jit(solution)/shard_map/all_to_all | solution.py:343
  18.3 0.0 copy-done.4
  18.3 0.4 plan.1
  18.7 18.3 %all-to-all-done = f32[16,1,4608]{2,1,0:T(1,128)S(1)} async-done(((f32[16,1,4608]{2,1,0:T(1,128)}), f32[16,1,4608]{2,1,0:T(1,128)S(1)}, u32[]{:S(2)}, u32[]{:S(2)}) %all-to-all-start) | async-done | bytes 294944 | tf_op jit(solution)/shard_map/all_to_all | solution.py:343
  37.0 0.3 lift.1
  37.4 17.9 %all_to_all.15 = f32[32,1,3328]{2,1,0:T(1,128)S(1)} all-to-all(f32[32,1,3328]{2,1,0:T(1,128)S(1)} %bitcast.15), channel_id=1, replica_groups=mesh['box'=32,'dir'=16] {'box'}, dimensions={0} | all-to-all | bytes 851968 | tf_op jit(solution)/shard_map/all_to_all | solution.py:381
  55.3 1.0 %lower.1 = f32[256,128]{1,0:T(8,128)} custom-call(bf16[128,512]{1,0:T(8,128)(2,1)S(1)} %get-tuple-element.8.picks, f32[2,32,128]{2,1,0:T(8,128)S(1)} %get-tuple-element.9.factors, f32[832,128]{1,0:T(8,128)S(1)} %bitcast.13), custom_call_target="tpu_custom_call" | custom-call | tf_op jit(solution)/shard_map/lower/pallas_call | solution.py:384
  56.2 6.8 %all-to-all-start.2 = ((f32[16,1,2048]{2,1,0:T(1,128)}), f32[16,1,2048]{2,1,0:T(1,128)S(1)}, u32[]{:S(2)}, u32[]{:S(2)}) async-start(f32[16,1,2048]{2,1,0:T(1,128)} %bitcast.9), calls=%async_computation.2 | async-start | bytes 262144 | tf_op jit(solution)/shard_map/all_to_all | solution.py:393
  63.0 1.5 %collective-permute-start = (f32[2,32,128]{2,1,0:T(8,128)S(1)}, f32[2,32,128]{2,1,0:T(8,128)S(1)}, u32[]{:S(2)}, u32[]{:S(2)}) collective-permute-start(f32[2,32,128]{2,1,0:T(8,128)S(1)} %copy-done.2), channel_id=1, source_target_pairs={{0,16},{16,32},{32,48},{48,64},{64,80},{80,96},{96,112},{112,128},... | collective-permute-start | bytes 98312 | tf_op jit(solution)/shard_map/ppermute | solution.py:320
  64.5 1.3 %collective-permute-start.1 = (f32[2,32,128]{2,1,0:T(8,128)S(1)}, f32[2,32,128]{2,1,0:T(8,128)S(1)}, u32[]{:S(2)}, u32[]{:S(2)}) collective-permute-start(f32[2,32,128]{2,1,0:T(8,128)S(1)} %copy-done.2), channel_id=1, source_target_pairs={{16,0},{32,16},{48,32},{64,48},{80,64},{96,80},{112,96},{128,112},... | collective-permute-start | bytes 98312 | tf_op jit(solution)/shard_map/ppermute | solution.py:321
  65.8 0.0 collective-permute-done.low
  65.8 2.5 %collective-permute-done.1.high = f32[2,32,128]{2,1,0:T(8,128)S(1)} collective-permute-done((f32[2,32,128]{2,1,0:T(8,128)S(1)}, f32[2,32,128]{2,1,0:T(8,128)S(1)}, u32[]{:S(2)}, u32[]{:S(2)}) %collective-permute-start.1) | collective-permute-done | bytes 32800 | tf_op jit(solution)/shard_map/ppermute | solution.py:321
  68.3 1.4 %copy-done.1 = f32[2,32,6,8,128]{4,3,2,1,0:T(8,128)S(1)} copy-done((f32[2,32,6,8,128]{4,3,2,1,0:T(8,128)S(1)}, f32[2,32,6,8,128]{4,3,2,1,0:T(8,128)}, u32[]{:S(2)}) %copy-start.1) | copy-done | bytes 1572888
  69.7 0.9 %near.1 = f32[2,32,8,128]{3,2,1,0:T(8,128)S(1)} custom-call(s32[6,32]{1,0:T(8,128)S(1)} %bitcast.24, s32[32]{0:T(128)S(1)} %copy-done.11, f32[2,32,128]{2,1,0:T(8,128)S(1)} %collective-permute-done.low, f32[2,32,128]{2,1,0:T(8,128)S(1)} %copy-done.2, f32[2,32,128]{2,1,0:T(8,128)S(1)} %collective-permute-done.1.high, f32[2,32,6,8,128]{4,3,2,1,0:T(8,128)S(1)} %copy-done.1), custom_call_target="tpu_custom_call" | custom-call | flops 4000000 | bytes 4000000 | tf_op jit(solution)/shard_map/near/pallas_call | solution.py:361
  70.6 6.4 %all-to-all-done.2 = f32[16,1,2048]{2,1,0:T(1,128)S(1)} async-done(((f32[16,1,2048]{2,1,0:T(1,128)}), f32[16,1,2048]{2,1,0:T(1,128)S(1)}, u32[]{:S(2)}, u32[]{:S(2)}) %all-to-all-start.2) | async-done | bytes 131104 | tf_op jit(solution)/shard_map/all_to_all | solution.py:393
  77.0 1.6 %field.1 = f32[2,8,32]{2,1,0:T(8,128)} custom-call(f32[256,128]{1,0:T(8,128)S(1)} %bitcast.17, f32[832,128]{1,0:T(8,128)S(1)} %bitcast.14, f32[2,2,32,8,512]{4,3,2,1,0:T(8,128)S(1)} %copy-done, f32[2,32,8,128]{3,2,1,0:T(8,128)S(1)} %near.1), custom_call_target="tpu_custom_call" | custom-call | tf_op jit(solution)/shard_map/field/pallas_call | solution.py:395
  (15 shorter events, 0.0 us)
Async XLA Ops:
  0.0 18.3 %copy-start.4 = (s32[128,4]{0,1:T(4,128)S(1)}, s32[128,4]{0,1:T(4,128)}, u32[]{:S(2)}) copy-start(s32[128,4]{0,1:T(4,128)} %param.17) | copy-start | bytes 6148
  0.0 18.3 %copy-start.5 = (f32[128,4]{0,1:T(4,128)S(1)}, f32[128,4]{0,1:T(4,128)}, u32[]{:S(2)}) copy-start(f32[128,4]{0,1:T(4,128)} %param.18) | copy-start | bytes 6148
  0.0 37.0 %copy-start.3 = (f32[2,8,128]{2,1,0:T(8,128)S(1)}, f32[2,8,128]{2,1,0:T(8,128)}, u32[]{:S(2)}) copy-start(f32[2,8,128]{2,1,0:T(8,128)} %shift.3) | copy-start | bytes 24580
  0.0 18.3 %copy-start.6 = (s32[128,16]{0,1:T(8,128)S(1)}, s32[128,16]{0,1:T(8,128)}, u32[]{:S(2)}) copy-start(s32[128,16]{0,1:T(8,128)} %param.20) | copy-start | bytes 24580
  0.0 18.3 %copy-start.7 = (s32[128,16]{0,1:T(8,128)S(1)}, s32[128,16]{0,1:T(8,128)}, u32[]{:S(2)}) copy-start(s32[128,16]{0,1:T(8,128)} %param.21) | copy-start | bytes 24580
  0.0 18.3 %copy-start.10 = (s32[128]{0:T(128)S(1)}, s32[128]{0:T(128)}, u32[]{:S(2)}) copy-start(s32[128]{0:T(128)} %param.22) | copy-start | bytes 1540
  0.0 18.3 %copy-start.8 = (f32[2,8,128]{2,1,0:T(8,128)S(1)}, f32[2,8,128]{2,1,0:T(8,128)}, u32[]{:S(2)}) copy-start(f32[2,8,128]{2,1,0:T(8,128)} %translation.1) | copy-start | bytes 24580
  2.9 60.2 %copy-start.2 = (f32[2,32,128]{2,1,0:T(8,128)S(1)}, f32[2,32,128]{2,1,0:T(8,128)}, u32[]{:S(2)}) copy-start(f32[2,32,128]{2,1,0:T(8,128)} %current.3) | copy-start | bytes 98308
  2.9 65.4 %copy-start.9 = (s32[32,6]{0,1:T(8,128)S(1)}, s32[32,6]{0,1:T(8,128)}, u32[]{:S(2)}) copy-start(s32[32,6]{0,1:T(8,128)} %param.14) | copy-start | bytes 2308
  2.9 65.4 %copy-start.11 = (s32[32]{0:T(128)S(1)}, s32[32]{0:T(128)}, u32[]{:S(2)}) copy-start(s32[32]{0:T(128)} %near_count.1) | copy-start | bytes 388
  2.9 34.1 %all-to-all-start = ((f32[16,1,4608]{2,1,0:T(1,128)}), f32[16,1,4608]{2,1,0:T(1,128)S(1)}, u32[]{:S(2)}, u32[]{:S(2)}) async-start(f32[16,1,4608]{2,1,0:T(1,128)} %bitcast.26), calls=%async_computation | async-start | bytes 589824 | tf_op jit(solution)/shard_map/all_to_all | solution.py:343
  37.0 39.9 %copy-start = (f32[2,2,32,8,512]{4,3,2,1,0:T(8,128)S(1)}, f32[2,2,32,8,512]{4,3,2,1,0:T(8,128)}, u32[]{:S(2)}) copy-start(f32[2,2,32,8,512]{4,3,2,1,0:T(8,128)} %radiation.3) | copy-start | bytes 6291460
  56.2 20.7 %all-to-all-start.2 = ((f32[16,1,2048]{2,1,0:T(1,128)}), f32[16,1,2048]{2,1,0:T(1,128)S(1)}, u32[]{:S(2)}, u32[]{:S(2)}) async-start(f32[16,1,2048]{2,1,0:T(1,128)} %bitcast.9), calls=%async_computation.2 | async-start | bytes 262144 | tf_op jit(solution)/shard_map/all_to_all | solution.py:393
  63.0 2.8 %collective-permute-start = (f32[2,32,128]{2,1,0:T(8,128)S(1)}, f32[2,32,128]{2,1,0:T(8,128)S(1)}, u32[]{:S(2)}, u32[]{:S(2)}) collective-permute-start(f32[2,32,128]{2,1,0:T(8,128)S(1)} %copy-done.2), channel_id=1, source_target_pairs={{0,16},{16,32},{32,48},{48,64},{64,80},{80,96},{96,112},{112,128},... | collective-permute-start | bytes 98312 | tf_op jit(solution)/shard_map/ppermute | solution.py:320
  64.5 3.8 %collective-permute-start.1 = (f32[2,32,128]{2,1,0:T(8,128)S(1)}, f32[2,32,128]{2,1,0:T(8,128)S(1)}, u32[]{:S(2)}, u32[]{:S(2)}) collective-permute-start(f32[2,32,128]{2,1,0:T(8,128)S(1)} %copy-done.2), channel_id=1, source_target_pairs={{16,0},{32,16},{48,32},{64,48},{80,64},{96,80},{112,96},{128,112},... | collective-permute-start | bytes 98312 | tf_op jit(solution)/shard_map/ppermute | solution.py:321
  68.3 1.4 %copy-start.1 = (f32[2,32,6,8,128]{4,3,2,1,0:T(8,128)S(1)}, f32[2,32,6,8,128]{4,3,2,1,0:T(8,128)}, u32[]{:S(2)}) copy-start(f32[2,32,6,8,128]{4,3,2,1,0:T(8,128)} %blocks.1) | copy-start | bytes 4718596

commit v7 on v5

--- a/solution.py
+++ b/solution.py
@@ -40,14 +40,15 @@
         pltpu.make_async_copy(source, target, sems.at[cuts + index])
         for index, (source, target) in enumerate(((current, given), (stencil, points), (weight, weights), (shift, shifts)))
     ]
-    for copy in small:
-        copy.start()
     copies = []
     for cut in range(cuts):
         part = pl.ds(cut * step, step)
         copy = pltpu.make_async_copy(radiation.at[:, :, part], patterns.at[:, :, part], sems.at[cut])
         copy.start()
         copies.append(copy)
+        if cut == 0:
+            for extra in small:
+                extra.start()
     for copy in small:
         copy.wait()
     for part in range(2):

time: 77.8 us -> 77.9 us (level)
  no operation moved by 1% of the time
where the time goes in v7:
time: 77.9 us; the launch traced here: 77.5 us
  blocking collectives  38.3 us (49%)
  starting transfers between devices  17.8 us (23%)
  waiting for transfers between devices  13.4 us (17%)
  Pallas kernels  6.41 us (8%)
  local copies, waits for them, and re-layouts  1.45 us (2%)
    all_to_all x1, blocking collectives, local(): lax.all_to_all(moved.reshape(dir_total, 1, lanes // 8 * share), 'dir', 0,...  20.5 us
    all_to_all x1, blocking collectives, local(): lax.all_to_all(tops.reshape(box_total, 1, height * share), 'box', 0, 0, t...  17.8 us
    all_to_all x1, starting transfers between devices, local(): lax.all_to_all(windows.reshape(dir_total, 1, (span + spare) * lanes), 'di...  15.2 us
    all_to_all x1, waiting for transfers between devices, local(): lax.all_to_all(windows.reshape(dir_total, 1, (span + spare) * lanes), 'di...  10.3 us
    ppermute x1, waiting for transfers between devices, local(): high = lax.ppermute(current, 'box', [(b, a) for a, b in forward])  3.06 us
    pallas_call x1, Pallas kernels, local(): pl.pallas_call(functools.partial(leaf_kernel, cuts, dir_total, box_total,...  2.9 us
    pallas_call x1, Pallas kernels, local(): pl.pallas_call(functools.partial(field_kernel, dir_total, box_total), out...  1.63 us
  transfers between devices with their start and end apart: 3, of which 2 were waited for; matrix products, arithmetic and copies ran while one was open for 0% of the time, Pallas kernels for 2%

profile of v7, /device:TPU:32, one launch (start us, length us, event | category | flops | bytes accessed | tf_op | source)
XLA Modules:
  0.0 77.5 jit_solution(17564906944055188288)
XLA Ops:
  0.0 0.0 copy-start.8
  0.0 0.0 copy-start.10
  0.0 0.0 copy-start.7
  0.0 0.0 copy-start.6
  0.0 0.0 copy-start.11
  0.1 0.0 copy-start.9
  0.1 0.0 copy-start.3
  0.1 2.9 %leaf.1 = f32[576,128]{1,0:T(8,128)} custom-call(f32[2,32,128]{2,1,0:T(8,128)} %current.3, s32[4,128]{1,0:T(4,128)} %bitcast.19, f32[4,128]{1,0:T(4,128)} %bitcast.21, f32[2,8,128]{2,1,0:T(8,128)} %shift.3, f32[2,2,32,8,512]{4,3,2,1,0:T(8,128)} %radiation.3), custom_call_target="tpu_custom_call" | custom-call | tf_op jit(solution)/shard_map/leaf/pallas_call | solution.py:325
  3.0 15.2 %all-to-all-start = ((f32[16,1,4608]{2,1,0:T(1,128)}), f32[16,1,4608]{2,1,0:T(1,128)S(1)}, u32[]{:S(2)}, u32[]{:S(2)}) async-start(f32[16,1,4608]{2,1,0:T(1,128)} %bitcast.27), calls=%async_computation | async-start | bytes 589824 | tf_op jit(solution)/shard_map/all_to_all | solution.py:345
  18.2 0.0 copy-done.2
  18.2 1.3 %collective-permute-start = (f32[2,32,128]{2,1,0:T(8,128)S(1)}, f32[2,32,128]{2,1,0:T(8,128)S(1)}, u32[]{:S(2)}, u32[]{:S(2)}) collective-permute-start(f32[2,32,128]{2,1,0:T(8,128)S(1)} %copy-done.2), channel_id=1, source_target_pairs={{0,16},{16,32},{32,48},{48,64},{64,80},{80,96},{96,112},{112,128},... | collective-permute-start | bytes 98312 | tf_op jit(solution)/shard_map/ppermute | solution.py:322
  19.5 1.3 %collective-permute-start.1 = (f32[2,32,128]{2,1,0:T(8,128)S(1)}, f32[2,32,128]{2,1,0:T(8,128)S(1)}, u32[]{:S(2)}, u32[]{:S(2)}) collective-permute-start(f32[2,32,128]{2,1,0:T(8,128)S(1)} %copy-done.2), channel_id=1, source_target_pairs={{16,0},{32,16},{48,32},{64,48},{80,64},{96,80},{112,96},{128,112},... | collective-permute-start | bytes 98312 | tf_op jit(solution)/shard_map/ppermute | solution.py:323
  20.9 0.4 plan.1
  21.3 0.0 collective-permute-done.low
  21.3 3.1 %collective-permute-done.1.high = f32[2,32,128]{2,1,0:T(8,128)S(1)} collective-permute-done((f32[2,32,128]{2,1,0:T(8,128)S(1)}, f32[2,32,128]{2,1,0:T(8,128)S(1)}, u32[]{:S(2)}, u32[]{:S(2)}) %collective-permute-start.1) | collective-permute-done | bytes 32800 | tf_op jit(solution)/shard_map/ppermute | solution.py:323
  24.3 1.4 %copy-done.1 = f32[2,32,6,8,128]{4,3,2,1,0:T(8,128)S(1)} copy-done((f32[2,32,6,8,128]{4,3,2,1,0:T(8,128)S(1)}, f32[2,32,6,8,128]{4,3,2,1,0:T(8,128)}, u32[]{:S(2)}) %copy-start.1) | copy-done | bytes 1572888
  25.8 0.9 %near.1 = f32[2,32,8,128]{3,2,1,0:T(8,128)S(1)} custom-call(s32[6,32]{1,0:T(8,128)S(1)} %bitcast.25, s32[32]{0:T(128)S(1)} %copy-done.11, f32[2,32,128]{2,1,0:T(8,128)S(1)} %collective-permute-done.low, f32[2,32,128]{2,1,0:T(8,128)S(1)} %copy-done.2, f32[2,32,128]{2,1,0:T(8,128)S(1)} %collective-permute-done.1.high, f32[2,32,6,8,128]{4,3,2,1,0:T(8,128)S(1)} %copy-done.1), custom_call_target="tpu_custom_call" | custom-call | flops 4000000 | bytes 4000000 | tf_op jit(solution)/shard_map/near/pallas_call | solution.py:363
  26.6 10.3 %all-to-all-done = f32[16,1,4608]{2,1,0:T(1,128)S(1)} async-done(((f32[16,1,4608]{2,1,0:T(1,128)}), f32[16,1,4608]{2,1,0:T(1,128)S(1)}, u32[]{:S(2)}, u32[]{:S(2)}) %all-to-all-start) | async-done | bytes 294944 | tf_op jit(solution)/shard_map/all_to_all | solution.py:345
  37.0 0.3 lift.1
  37.3 17.8 %all_to_all.15 = f32[32,1,3328]{2,1,0:T(1,128)S(1)} all-to-all(f32[32,1,3328]{2,1,0:T(1,128)S(1)} %bitcast.15), channel_id=1, replica_groups=mesh['box'=32,'dir'=16] {'box'}, dimensions={0} | all-to-all | bytes 851968 | tf_op jit(solution)/shard_map/all_to_all | solution.py:383
  55.1 0.3 lower.1
  55.4 20.5 %all_to_all.16 = f32[16,1,2048]{2,1,0:T(1,128)S(1)} all-to-all(f32[16,1,2048]{2,1,0:T(1,128)S(1)} %bitcast.18), channel_id=1, replica_groups=mesh['box'=32,'dir'=16] {'dir'}, dimensions={0} | all-to-all | bytes 262144 | tf_op jit(solution)/shard_map/all_to_all | solution.py:395
  75.9 0.0 copy-done
  75.9 1.6 %field.1 = f32[2,8,32]{2,1,0:T(8,128)} custom-call(f32[256,128]{1,0:T(8,128)S(1)} %bitcast.17, f32[832,128]{1,0:T(8,128)S(1)} %bitcast.14, f32[2,2,32,8,512]{4,3,2,1,0:T(8,128)S(1)} %copy-done, f32[2,32,8,128]{3,2,1,0:T(8,128)S(1)} %near.1), custom_call_target="tpu_custom_call" | custom-call | tf_op jit(solution)/shard_map/field/pallas_call | solution.py:397
  (14 shorter events, 0.0 us)
Async XLA Ops:
  0.0 18.2 %copy-start.2 = (f32[2,32,128]{2,1,0:T(8,128)S(1)}, f32[2,32,128]{2,1,0:T(8,128)}, u32[]{:S(2)}) copy-start(f32[2,32,128]{2,1,0:T(8,128)} %current.3) | copy-start | bytes 98308
  0.0 20.8 %copy-start.5 = (f32[128,4]{0,1:T(4,128)S(1)}, f32[128,4]{0,1:T(4,128)}, u32[]{:S(2)}) copy-start(f32[128,4]{0,1:T(4,128)} %param.18) | copy-start | bytes 6148
  0.0 20.8 %copy-start.4 = (s32[128,4]{0,1:T(4,128)S(1)}, s32[128,4]{0,1:T(4,128)}, u32[]{:S(2)}) copy-start(s32[128,4]{0,1:T(4,128)} %param.17) | copy-start | bytes 6148
  0.0 20.8 %copy-start.8 = (f32[2,8,128]{2,1,0:T(8,128)S(1)}, f32[2,8,128]{2,1,0:T(8,128)}, u32[]{:S(2)}) copy-start(f32[2,8,128]{2,1,0:T(8,128)} %translation.1) | copy-start | bytes 24580
  0.0 20.8 %copy-start.10 = (s32[128]{0:T(128)S(1)}, s32[128]{0:T(128)}, u32[]{:S(2)}) copy-start(s32[128]{0:T(128)} %param.22) | copy-start | bytes 1540
  0.0 20.8 %copy-start.7 = (s32[128,16]{0,1:T(8,128)S(1)}, s32[128,16]{0,1:T(8,128)}, u32[]{:S(2)}) copy-start(s32[128,16]{0,1:T(8,128)} %param.21) | copy-start | bytes 24580
  0.0 20.8 %copy-start.6 = (s32[128,16]{0,1:T(8,128)S(1)}, s32[128,16]{0,1:T(8,128)}, u32[]{:S(2)}) copy-start(s32[128,16]{0,1:T(8,128)} %param.20) | copy-start | bytes 24580
  0.0 24.3 %copy-start.11 = (s32[32]{0:T(128)S(1)}, s32[32]{0:T(128)}, u32[]{:S(2)}) copy-start(s32[32]{0:T(128)} %near_count.1) | copy-start | bytes 388
  0.1 24.3 %copy-start.9 = (s32[32,6]{0,1:T(8,128)S(1)}, s32[32,6]{0,1:T(8,128)}, u32[]{:S(2)}) copy-start(s32[32,6]{0,1:T(8,128)} %param.14) | copy-start | bytes 2308
  0.1 36.9 %copy-start.3 = (f32[2,8,128]{2,1,0:T(8,128)S(1)}, f32[2,8,128]{2,1,0:T(8,128)}, u32[]{:S(2)}) copy-start(f32[2,8,128]{2,1,0:T(8,128)} %shift.3) | copy-start | bytes 24580
  3.0 34.0 %all-to-all-start = ((f32[16,1,4608]{2,1,0:T(1,128)}), f32[16,1,4608]{2,1,0:T(1,128)S(1)}, u32[]{:S(2)}, u32[]{:S(2)}) async-start(f32[16,1,4608]{2,1,0:T(1,128)} %bitcast.27), calls=%async_computation | async-start | bytes 589824 | tf_op jit(solution)/shard_map/all_to_all | solution.py:345
  18.2 3.1 %collective-permute-start = (f32[2,32,128]{2,1,0:T(8,128)S(1)}, f32[2,32,128]{2,1,0:T(8,128)S(1)}, u32[]{:S(2)}, u32[]{:S(2)}) collective-permute-start(f32[2,32,128]{2,1,0:T(8,128)S(1)} %copy-done.2), channel_id=1, source_target_pairs={{0,16},{16,32},{32,48},{48,64},{64,80},{80,96},{96,112},{112,128},... | collective-permute-start | bytes 98312 | tf_op jit(solution)/shard_map/ppermute | solution.py:322
  19.5 4.8 %collective-permute-start.1 = (f32[2,32,128]{2,1,0:T(8,128)S(1)}, f32[2,32,128]{2,1,0:T(8,128)S(1)}, u32[]{:S(2)}, u32[]{:S(2)}) collective-permute-start(f32[2,32,128]{2,1,0:T(8,128)S(1)} %copy-done.2), channel_id=1, source_target_pairs={{16,0},{32,16},{48,32},{64,48},{80,64},{96,80},{112,96},{128,112},... | collective-permute-start | bytes 98312 | tf_op jit(solution)/shard_map/ppermute | solution.py:323
  24.3 1.4 %copy-start.1 = (f32[2,32,6,8,128]{4,3,2,1,0:T(8,128)S(1)}, f32[2,32,6,8,128]{4,3,2,1,0:T(8,128)}, u32[]{:S(2)}) copy-start(f32[2,32,6,8,128]{4,3,2,1,0:T(8,128)} %blocks.1) | copy-start | bytes 4718596
  25.8 50.1 %copy-start = (f32[2,2,32,8,512]{4,3,2,1,0:T(8,128)S(1)}, f32[2,2,32,8,512]{4,3,2,1,0:T(8,128)}, u32[]{:S(2)}) copy-start(f32[2,2,32,8,512]{4,3,2,1,0:T(8,128)} %radiation.3) | copy-start | bytes 6291460

commit v8 on v5

--- a/solution.py
+++ b/solution.py
@@ -1,4 +1,5 @@
 import functools
+import math
 
 import jax
 import jax.numpy as jnp
@@ -128,7 +129,7 @@
             factors[part, which * parents : (which + 1) * parents, :] = jnp.broadcast_to(one, (parents, lanes))
 
 
-def lift_kernel(shares, copies, spare, received, interp, shift, near, out, total, tops):
+def lift_kernel(shares, copies, spare, received, interp, shift, near, out, total, tops, group):
     each = received.shape[0] // shares
     span = each - spare
     total[...] = jnp.zeros_like(total)
@@ -152,8 +153,12 @@
         at = share * each + span + (number - share * (16 + reach)) // copies
         tops[2 * lines + index : 2 * lines + index + 1, :] = received[pl.ds(at, 1), :]
     value = tops[...]
-    for copy in range(copies):
-        out[copy * height : (copy + 1) * height, :] = value
+    several = group.shape[0] // height
+    for copy in range(several):
+        group[copy * height : (copy + 1) * height, :] = value
+    tiles = group[...]
+    for copy in range(copies // several):
+        out[copy * several * height : (copy + 1) * several * height, :] = tiles
 
 
 def lower_kernel(shares, parents, picks, factors, gathered, out, compact):
@@ -375,7 +380,11 @@
         out_shape=shape((box_total * height, share)),
         in_specs=[VMEM] * 3 + [ANY],
         out_specs=VMEM,
-        scratch_shapes=[pltpu.VMEM((128, lanes), f32), pltpu.VMEM((height, share), f32)],
+        scratch_shapes=[
+            pltpu.VMEM((128, lanes), f32),
+            pltpu.VMEM((height, share), f32),
+            pltpu.VMEM((height * math.gcd(box_total, 8 // math.gcd(height, 8)), share), f32),
+        ],
         compiler_params=params,
         name="lift",
     )(windows.reshape(dir_total * (span + spare), lanes), interp, child_shift, near)

time: 77.8 us -> 77.8 us (level)
  no operation moved by 1% of the time
where the time goes in v8:
time: 77.8 us; the launch traced here: 77.5 us
  blocking collectives  38.3 us (49%)
  starting transfers between devices  17.8 us (23%)
  waiting for transfers between devices  13.4 us (17%)
  Pallas kernels  6.33 us (8%)
  local copies, waits for them, and re-layouts  1.45 us (2%)
    all_to_all x1, blocking collectives, local(): lax.all_to_all(moved.reshape(dir_total, 1, lanes // 8 * share), 'dir', 0,...  20.5 us
    all_to_all x1, blocking collectives, local(): lax.all_to_all(tops.reshape(box_total, 1, height * share), 'box', 0, 0, t...  17.8 us
    all_to_all x1, starting transfers between devices, local(): lax.all_to_all(windows.reshape(dir_total, 1, (span + spare) * lanes), 'di...  15.2 us
    all_to_all x1, waiting for transfers between devices, local(): lax.all_to_all(windows.reshape(dir_total, 1, (span + spare) * lanes), 'di...  10.3 us
    ppermute x1, waiting for transfers between devices, local(): high = lax.ppermute(current, 'box', [(b, a) for a, b in forward])  3.06 us
    pallas_call x1, Pallas kernels, local(): pl.pallas_call(functools.partial(leaf_kernel, cuts, dir_total, box_total,...  2.81 us
    pallas_call x1, Pallas kernels, local(): pl.pallas_call(functools.partial(field_kernel, dir_total, box_total), out...  1.63 us
  transfers between devices with their start and end apart: 3, of which 2 were waited for; matrix products, arithmetic and copies ran while one was open for 0% of the time, Pallas kernels for 2%

profile of v8, /device:TPU:32, one launch (start us, length us, event | category | flops | bytes accessed | tf_op | source)
XLA Modules:
  0.0 77.5 jit_solution(2476216019152016167)
XLA Ops:
  0.0 0.0 copy-start.8
  0.0 0.0 copy-start.10
  0.0 0.0 copy-start.7
  0.0 0.0 copy-start.6
  0.0 0.0 copy-start.11
  0.1 0.0 copy-start.9
  0.1 0.0 copy-start.3
  0.1 2.8 %leaf.1 = f32[576,128]{1,0:T(8,128)} custom-call(f32[2,32,128]{2,1,0:T(8,128)} %current.3, s32[4,128]{1,0:T(4,128)} %bitcast.19, f32[4,128]{1,0:T(4,128)} %bitcast.21, f32[2,8,128]{2,1,0:T(8,128)} %shift.3, f32[2,2,32,8,512]{4,3,2,1,0:T(8,128)} %radiation.3), custom_call_target="tpu_custom_call" | custom-call | tf_op jit(solution)/shard_map/leaf/pallas_call | solution.py:329
  2.9 15.2 %all-to-all-start = ((f32[16,1,4608]{2,1,0:T(1,128)}), f32[16,1,4608]{2,1,0:T(1,128)S(1)}, u32[]{:S(2)}, u32[]{:S(2)}) async-start(f32[16,1,4608]{2,1,0:T(1,128)} %bitcast.27), calls=%async_computation | async-start | bytes 589824 | tf_op jit(solution)/shard_map/all_to_all | solution.py:349
  18.1 0.0 copy-done.2
  18.1 1.3 %collective-permute-start = (f32[2,32,128]{2,1,0:T(8,128)S(1)}, f32[2,32,128]{2,1,0:T(8,128)S(1)}, u32[]{:S(2)}, u32[]{:S(2)}) collective-permute-start(f32[2,32,128]{2,1,0:T(8,128)S(1)} %copy-done.2), channel_id=1, source_target_pairs={{0,16},{16,32},{32,48},{48,64},{64,80},{80,96},{96,112},{112,128},... | collective-permute-start | bytes 98312 | tf_op jit(solution)/shard_map/ppermute | solution.py:326
  19.4 1.3 %collective-permute-start.1 = (f32[2,32,128]{2,1,0:T(8,128)S(1)}, f32[2,32,128]{2,1,0:T(8,128)S(1)}, u32[]{:S(2)}, u32[]{:S(2)}) collective-permute-start(f32[2,32,128]{2,1,0:T(8,128)S(1)} %copy-done.2), channel_id=1, source_target_pairs={{16,0},{32,16},{48,32},{64,48},{80,64},{96,80},{112,96},{128,112},... | collective-permute-start | bytes 98312 | tf_op jit(solution)/shard_map/ppermute | solution.py:327
  20.7 0.0 copy-done.5
  20.8 0.4 plan.1
  21.2 0.0 collective-permute-done.low
  21.2 3.1 %collective-permute-done.1.high = f32[2,32,128]{2,1,0:T(8,128)S(1)} collective-permute-done((f32[2,32,128]{2,1,0:T(8,128)S(1)}, f32[2,32,128]{2,1,0:T(8,128)S(1)}, u32[]{:S(2)}, u32[]{:S(2)}) %collective-permute-start.1) | collective-permute-done | bytes 32800 | tf_op jit(solution)/shard_map/ppermute | solution.py:327
  24.3 1.4 %copy-done.1 = f32[2,32,6,8,128]{4,3,2,1,0:T(8,128)S(1)} copy-done((f32[2,32,6,8,128]{4,3,2,1,0:T(8,128)S(1)}, f32[2,32,6,8,128]{4,3,2,1,0:T(8,128)}, u32[]{:S(2)}) %copy-start.1) | copy-done | bytes 1572888
  25.7 0.9 %near.1 = f32[2,32,8,128]{3,2,1,0:T(8,128)S(1)} custom-call(s32[6,32]{1,0:T(8,128)S(1)} %bitcast.25, s32[32]{0:T(128)S(1)} %copy-done.11, f32[2,32,128]{2,1,0:T(8,128)S(1)} %collective-permute-done.low, f32[2,32,128]{2,1,0:T(8,128)S(1)} %copy-done.2, f32[2,32,128]{2,1,0:T(8,128)S(1)} %collective-permute-done.1.high, f32[2,32,6,8,128]{4,3,2,1,0:T(8,128)S(1)} %copy-done.1), custom_call_target="tpu_custom_call" | custom-call | flops 4000000 | bytes 4000000 | tf_op jit(solution)/shard_map/near/pallas_call | solution.py:367
  26.6 10.3 %all-to-all-done = f32[16,1,4608]{2,1,0:T(1,128)S(1)} async-done(((f32[16,1,4608]{2,1,0:T(1,128)}), f32[16,1,4608]{2,1,0:T(1,128)S(1)}, u32[]{:S(2)}, u32[]{:S(2)}) %all-to-all-start) | async-done | bytes 294944 | tf_op jit(solution)/shard_map/all_to_all | solution.py:349
  36.9 0.3 lift.1
  37.2 17.8 %all_to_all.15 = f32[32,1,3328]{2,1,0:T(1,128)S(1)} all-to-all(f32[32,1,3328]{2,1,0:T(1,128)S(1)} %bitcast.15), channel_id=1, replica_groups=mesh['box'=32,'dir'=16] {'box'}, dimensions={0} | all-to-all | bytes 851968 | tf_op jit(solution)/shard_map/all_to_all | solution.py:391
  55.0 0.3 lower.1
  55.3 20.5 %all_to_all.16 = f32[16,1,2048]{2,1,0:T(1,128)S(1)} all-to-all(f32[16,1,2048]{2,1,0:T(1,128)S(1)} %bitcast.18), channel_id=1, replica_groups=mesh['box'=32,'dir'=16] {'dir'}, dimensions={0} | all-to-all | bytes 262144 | tf_op jit(solution)/shard_map/all_to_all | solution.py:403
  75.8 1.6 %field.1 = f32[2,8,32]{2,1,0:T(8,128)} custom-call(f32[256,128]{1,0:T(8,128)S(1)} %bitcast.17, f32[832,128]{1,0:T(8,128)S(1)} %bitcast.14, f32[2,2,32,8,512]{4,3,2,1,0:T(8,128)S(1)} %copy-done, f32[2,32,8,128]{3,2,1,0:T(8,128)S(1)} %near.1), custom_call_target="tpu_custom_call" | custom-call | tf_op jit(solution)/shard_map/field/pallas_call | solution.py:405
  (14 shorter events, 0.0 us)
Async XLA Ops:
  0.0 18.1 %copy-start.2 = (f32[2,32,128]{2,1,0:T(8,128)S(1)}, f32[2,32,128]{2,1,0:T(8,128)}, u32[]{:S(2)}) copy-start(f32[2,32,128]{2,1,0:T(8,128)} %current.3) | copy-start | bytes 98308
  0.0 20.7 %copy-start.5 = (f32[128,4]{0,1:T(4,128)S(1)}, f32[128,4]{0,1:T(4,128)}, u32[]{:S(2)}) copy-start(f32[128,4]{0,1:T(4,128)} %param.18) | copy-start | bytes 6148
  0.0 20.7 %copy-start.4 = (s32[128,4]{0,1:T(4,128)S(1)}, s32[128,4]{0,1:T(4,128)}, u32[]{:S(2)}) copy-start(s32[128,4]{0,1:T(4,128)} %param.17) | copy-start | bytes 6148
  0.0 20.7 %copy-start.8 = (f32[2,8,128]{2,1,0:T(8,128)S(1)}, f32[2,8,128]{2,1,0:T(8,128)}, u32[]{:S(2)}) copy-start(f32[2,8,128]{2,1,0:T(8,128)} %translation.1) | copy-start | bytes 24580
  0.0 20.7 %copy-start.10 = (s32[128]{0:T(128)S(1)}, s32[128]{0:T(128)}, u32[]{:S(2)}) copy-start(s32[128]{0:T(128)} %param.22) | copy-start | bytes 1540
  0.0 20.7 %copy-start.7 = (s32[128,16]{0,1:T(8,128)S(1)}, s32[128,16]{0,1:T(8,128)}, u32[]{:S(2)}) copy-start(s32[128,16]{0,1:T(8,128)} %param.21) | copy-start | bytes 24580
  0.0 20.7 %copy-start.6 = (s32[128,16]{0,1:T(8,128)S(1)}, s32[128,16]{0,1:T(8,128)}, u32[]{:S(2)}) copy-start(s32[128,16]{0,1:T(8,128)} %param.20) | copy-start | bytes 24580
  0.0 24.2 %copy-start.11 = (s32[32]{0:T(128)S(1)}, s32[32]{0:T(128)}, u32[]{:S(2)}) copy-start(s32[32]{0:T(128)} %near_count.1) | copy-start | bytes 388
  0.1 24.2 %copy-start.9 = (s32[32,6]{0,1:T(8,128)S(1)}, s32[32,6]{0,1:T(8,128)}, u32[]{:S(2)}) copy-start(s32[32,6]{0,1:T(8,128)} %param.14) | copy-start | bytes 2308
  0.1 36.8 %copy-start.3 = (f32[2,8,128]{2,1,0:T(8,128)S(1)}, f32[2,8,128]{2,1,0:T(8,128)}, u32[]{:S(2)}) copy-start(f32[2,8,128]{2,1,0:T(8,128)} %shift.3) | copy-start | bytes 24580
  2.9 34.0 %all-to-all-start = ((f32[16,1,4608]{2,1,0:T(1,128)}), f32[16,1,4608]{2,1,0:T(1,128)S(1)}, u32[]{:S(2)}, u32[]{:S(2)}) async-start(f32[16,1,4608]{2,1,0:T(1,128)} %bitcast.27), calls=%async_computation | async-start | bytes 589824 | tf_op jit(solution)/shard_map/all_to_all | solution.py:349
  18.1 3.1 %collective-permute-start = (f32[2,32,128]{2,1,0:T(8,128)S(1)}, f32[2,32,128]{2,1,0:T(8,128)S(1)}, u32[]{:S(2)}, u32[]{:S(2)}) collective-permute-start(f32[2,32,128]{2,1,0:T(8,128)S(1)} %copy-done.2), channel_id=1, source_target_pairs={{0,16},{16,32},{32,48},{48,64},{64,80},{80,96},{96,112},{112,128},... | collective-permute-start | bytes 98312 | tf_op jit(solution)/shard_map/ppermute | solution.py:326
  19.4 4.8 %collective-permute-start.1 = (f32[2,32,128]{2,1,0:T(8,128)S(1)}, f32[2,32,128]{2,1,0:T(8,128)S(1)}, u32[]{:S(2)}, u32[]{:S(2)}) collective-permute-start(f32[2,32,128]{2,1,0:T(8,128)S(1)} %copy-done.2), channel_id=1, source_target_pairs={{16,0},{32,16},{48,32},{64,48},{80,64},{96,80},{112,96},{128,112},... | collective-permute-start | bytes 98312 | tf_op jit(solution)/shard_map/ppermute | solution.py:327
  24.3 1.4 %copy-start.1 = (f32[2,32,6,8,128]{4,3,2,1,0:T(8,128)S(1)}, f32[2,32,6,8,128]{4,3,2,1,0:T(8,128)}, u32[]{:S(2)}) copy-start(f32[2,32,6,8,128]{4,3,2,1,0:T(8,128)} %blocks.1) | copy-start | bytes 4718596
  25.7 50.1 %copy-start = (f32[2,2,32,8,512]{4,3,2,1,0:T(8,128)S(1)}, f32[2,2,32,8,512]{4,3,2,1,0:T(8,128)}, u32[]{:S(2)}) copy-start(f32[2,2,32,8,512]{4,3,2,1,0:T(8,128)} %radiation.3) | copy-start | bytes 6291460
